TPU v7x, 32 devices: a whole 2x2x4 slice. The times are simulated.
32 devices in a mesh: gen: 4 (over z), user: 4 (over y, x), cand: 2 (over core).
Axes of the slice: x: 2, y: 2, z: 4, core: 2. Of those that a mesh axis runs over, the one named last changes fastest.
Arguments:
- states: bfloat16 [4096, 4096], P(('user', 'cand')), may hold values from -6 to 6
- norm_gain: float32 [4096], replicated, may hold values from 0.1 to 1.9
- gate_weight: bfloat16 [4096, 7168], P('user', 'gen'), may hold values from -0.09375 to 0.09375
- up_weight: bfloat16 [4096, 7168], P('user', 'gen'), may hold values from -0.09375 to 0.09375
- down_weight: bfloat16 [7168, 4096], P('gen', 'user'), may hold values from -0.0625 to 0.0625
- proj_weight: bfloat16 [4096, 1024], P('gen'), may hold values from -0.09375 to 0.09375
- private_rows: bfloat16 [4096, 1024], P(('gen', 'user')), may hold values from -6 to 6
- enc_weight: bfloat16 [1024, 1024], replicated, may hold values from -0.1875 to 0.1875
- user_ids: int32 [4096], P(('gen', 'user')), may hold values from 0 to 31
Outputs:
- votes: float32 [4, 2, 128], P(None, 'cand')
Inputs may be any that keep to these rules, and one draw needn't show every extreme that they name: `user_ids`: a user is a pair of a block of 256 rows and a slot; no user has rows in two blocks.
All inputs are finite; a program needn't handle non-finite values.
Results may differ from a plain program's by a relative error of at most 0.0025.
Values may be sent and summed in bfloat16 or wider, within the bound.
A program may use at most 128 MiB of HBM per device.

v0:
```python
import jax
import jax.numpy as jnp
from jax import lax
from jax.sharding import PartitionSpec as P

STEPS = 4
CAP = 8
USERS_DEV = 32


def unit_rows(matrix):
    return (matrix * lax.rsqrt(jnp.sum(matrix * matrix, axis=1, keepdims=True) + 1e-06)).astype(
        jnp.bfloat16
    )


def project_in(inputs, gate_part, up_part):

    def add_rows(piece):
        return jnp.dot(inputs, piece, preferred_element_type=jnp.float32)

    gate = add_rows(lax.all_gather(gate_part, "user", axis=0, tiled=True))
    up_proj = add_rows(lax.all_gather(up_part, "user", axis=0, tiled=True))
    return (gate, up_proj)


def shards(
    states,
    norm_gain,
    gate_weight,
    up_weight,
    down_weight,
    proj_weight,
    private_rows,
    enc_weight,
    user_ids,
):
    tok_rows, width_model = states.shape
    groups = tok_rows // STEPS
    values = states.astype(jnp.float32)
    normed = (
        values * lax.rsqrt(jnp.mean(values * values, axis=1, keepdims=True) + 1e-05) * norm_gain
    ).astype(jnp.bfloat16)
    partners = lax.axis_size("cand")
    own_part = lax.axis_index("cand")
    part_width = gate_weight.shape[1] // partners
    gate_part = lax.dynamic_slice_in_dim(gate_weight, own_part * part_width, part_width, 1)
    up_part = lax.dynamic_slice_in_dim(up_weight, own_part * part_width, part_width, 1)
    down_part = lax.dynamic_slice_in_dim(down_weight, own_part * part_width, part_width, 0)
    inputs = lax.all_gather(normed, "cand", axis=0, tiled=True)
    gate, up_proj = project_in(inputs, gate_part, up_part)
    hidden = (jax.nn.silu(gate) * up_proj).astype(jnp.bfloat16)
    mixed = jnp.dot(
        hidden,
        lax.all_gather(down_part, "user", axis=1, tiled=True),
        preferred_element_type=jnp.float32,
    )
    pooled_mlp = jnp.sum(mixed.reshape(-1, STEPS, width_model), axis=1)
    pooled_mlp = lax.psum_scatter(pooled_mlp, "cand", scatter_dimension=0, tiled=True)
    pooled_mlp = lax.psum_scatter(pooled_mlp, "gen", scatter_dimension=1, tiled=True)
    slab_width = pooled_mlp.shape[1]
    own_cols = lax.dynamic_slice_in_dim(values, lax.axis_index("gen") * slab_width, slab_width, 1)
    pooled_in = jnp.sum(own_cols.reshape(groups, STEPS, slab_width), axis=1)
    pooled = ((pooled_in + pooled_mlp) / STEPS).astype(jnp.bfloat16)
    partial_emb = jnp.dot(pooled, proj_weight, preferred_element_type=jnp.float32)
    embedding = lax.psum(partial_emb, "gen")
    candidate = unit_rows(embedding)
    every_cand = lax.all_gather(candidate, "user", axis=0, tiled=True)
    encoded = unit_rows(jnp.dot(private_rows, enc_weight, preferred_element_type=jnp.float32))
    scores = lax.dot_general(
        encoded, every_cand, (((1,), (1,)), ((), ())), preferred_element_type=jnp.float32
    )
    kernel = jnp.exp(scores * 60.0)
    totals = lax.psum(jnp.sum(kernel, axis=1), "cand")
    member = (user_ids[:, None] == jnp.arange(USERS_DEV, dtype=jnp.int32)[None, :]).astype(
        jnp.float32
    )
    counts = jnp.sum(member, axis=0)
    limit = jnp.minimum(1.0, CAP / jnp.maximum(counts, 1.0))
    row_cap = jnp.dot(member, limit, precision=lax.Precision.HIGHEST)
    row_total = private_rows.shape[0] * lax.axis_size("gen") * lax.axis_size("user")
    cand_total = every_cand.shape[0] * lax.axis_size("cand")
    weight_rows = row_cap / totals * (cand_total / row_total)
    partial_votes = jnp.dot(weight_rows, kernel, precision=lax.Precision.HIGHEST)
    votes = lax.psum(partial_votes, ("gen", "user"))
    return votes.reshape(lax.axis_size("user"), 1, groups)


def solution(mesh):
    return jax.shard_map(
        shards,
        mesh=mesh,
        in_specs=(
            P(("user", "cand"), None),
            P(),
            P("user", "gen"),
            P("user", "gen"),
            P("gen", "user"),
            P("gen", None),
            P(("gen", "user"), None),
            P(),
            P(("gen", "user")),
        ),
        out_specs=P(None, "cand", None),
        check_vma=False,
    )
```

profile of v0, /device:TPU:0, one launch (start us, length us, event | category | flops | bytes accessed | tf_op | source)
XLA Modules:
  0.0 527.4 jit_solution(11088891279961570723)
XLA Ops:
  6.5 3.2 multiply_reduce_fusion
  9.8 0.4 copy-done.1
  10.1 4.4 multiply_convert_fusion
  14.6 2.9 constant_dynamic-slice_fusion.2
  17.6 3.0 constant_dynamic-slice_fusion.1
  20.6 2.9 constant_dynamic-slice_fusion
  23.5 0.2 reduce-scatter.3.cloned.1.call-start
  23.8 13.5 %all-gather.6.cloned.1.call-done = bf16[1024,4096]{1,0:T(8,128)(2,1)} async-done(((bf16[512,4096]{1,0:T(8,128)(2,1)}), bf16[1024,4096]{1,0:T(8,128)(2,1)}) %all-gather.6.cloned.1.call-update) | async-done | bytes 8388624 | tf_op jit(solution)/shard_map/all_gather | solution.py:50
  37.3 81.9 %all-gather.8.cloned.1.call-done = bf16[4096,896]{1,0:T(8,128)(2,1)} async-done(((bf16[1024,896]{1,0:T(8,128)(2,1)}), bf16[4096,896]{1,0:T(8,128)(2,1)}) %all-gather.8.cloned.1.call-update) | async-done | bytes 7340048 | tf_op jit(solution)/shard_map/all_gather | solution.py:22
  119.2 14.6 %fusion.17 = f32[1024,896]{1,0:T(8,128)} fusion(bf16[1024,4096]{1,0:T(8,128)(2,1)} %all-gather.6.cloned.1.call-done, bf16[4096,896]{1,0:T(8,128)(2,1)} %all-gather.8.cloned.1.call-done), kind=kOutput, calls=%fused_computation.38 | convolution fusion | flops 7516192768 | bytes 19398656 | tf_op jit(solution)/shard_map/dot_general | solution.py:20
  133.8 66.2 %all-gather.10.cloned.1.call-done = bf16[4096,896]{1,0:T(8,128)(2,1)} async-done(((bf16[1024,896]{1,0:T(8,128)(2,1)}), bf16[4096,896]{1,0:T(8,128)(2,1)}) %all-gather.10.cloned.1.call-update) | async-done | bytes 7340048 | tf_op jit(solution)/shard_map/all_gather | solution.py:23
  200.0 80.6 %all-gather.12.cloned.1.call-done = bf16[896,4096]{1,0:T(8,128)(2,1)} async-done(((bf16[896,1024]{1,0:T(8,128)(2,1)}), bf16[896,4096]{1,0:T(8,128)(2,1)}) %all-gather.12.cloned.1.call-update) | async-done | bytes 7340048 | tf_op jit(solution)/shard_map/all_gather | solution.py:55
  280.6 27.9 %fusion = f32[1024,4096]{1,0:T(8,128)} fusion(bf16[896,4096]{1,0:T(8,128)(2,1)} %all-gather.12.cloned.1.call-done, f32[1024,896]{1,0:T(8,128)} %fusion.17, bf16[1024,4096]{1,0:T(8,128)(2,1)} %all-gather.6.cloned.1.call-done, bf16[4096,896]{1,0:T(8,128)(2,1)} %all-gather.10.cloned.1.call-done), kind=kOutput, calls=%fused_computation.3 | convolution fusion | flops 15037890560 | bytes 43515904 | tf_op jit(solution)/shard_map/dot_general | solution.py:53
  308.6 19.0 %reshape.32 = f32[256,4,4096]{2,1,0:T(4,128)} reshape(f32[1024,4096]{1,0:T(8,128)} %fusion) | data formatting | bytes 33554432 | tf_op jit(solution)/shard_map/reshape | solution.py:58
  327.6 15.0 %reduce_sum.67 = f32[256,4096]{1,0:T(8,128)} reduce(f32[256,4,4096]{2,1,0:T(4,128)} %reshape.32, f32[]{:T(128)} %constant.16.clone.1), dimensions={1}, to_apply=%region_4.5 | reduce | flops 3145728 | bytes 20971524 | tf_op jit(solution)/shard_map/reduce_sum | solution.py:58
  342.7 12.1 %reduce-scatter.3.cloned.1.call-done = f32[128,4096]{1,0:T(8,128)} async-done(((f32[256,4096]{1,0:T(8,128)}), f32[128,4096]{1,0:T(8,128)}) %reduce-scatter.3.cloned.1.call-update) | async-done | bytes 2097168 | tf_op jit(solution)/shard_map/reduce_scatter | solution.py:59
  354.8 0.3 all-reduce.2.cloned.1.call-start
  355.1 6.5 %convert_element_type.23 = f32[512,4096]{1,0:T(8,128)} convert(bf16[512,4096]{1,0:T(8,128)(2,1)} %param.9) | non-fusion elementwise | flops 2097152 | bytes 12582912 | tf_op jit(solution)/shard_map/convert_element_type | solution.py:40
  361.6 3.1 constant_dynamic-slice_fusion.3
  364.7 2.9 reshape.31
  367.6 2.9 reduce_sum.65
  370.5 31.7 %reduce-scatter.5.cloned.1.call-done = f32[128,1024]{1,0:T(8,128)} async-done(((f32[128,4096]{1,0:T(8,128)}), f32[128,1024]{1,0:T(8,128)}) %reduce-scatter.5.cloned.1.call-update) | async-done | bytes 524304 | tf_op jit(solution)/shard_map/reduce_scatter | solution.py:60
  402.2 3.0 fusion.4
  405.3 37.7 %all-reduce.2.cloned.1.call-done = f32[128,1024]{1,0:T(8,128)} async-done(((f32[128,1024]{1,0:T(8,128)}), f32[128,1024]{1,0:T(8,128)}) %all-reduce.2.cloned.1.call-update) | async-done | bytes 524304 | tf_op jit(solution)/shard_map/psum | solution.py:66
  443.0 1.2 multiply_reduce_fusion.2
  444.2 1.9 multiply_convert_fusion.4
  446.2 1.8 multiply_reduce_fusion.1
  448.2 24.7 %all-gather.14.cloned.1.call-done = bf16[512,1024]{1,0:T(8,128)(2,1)} async-done(((bf16[128,1024]{1,0:T(8,128)(2,1)}), bf16[512,1024]{1,0:T(8,128)(2,1)}) %all-gather.14.cloned.1.call-update) | async-done | bytes 1048592 | tf_op jit(solution)/shard_map/all_gather | solution.py:68
  472.8 2.5 fusion.16
  475.4 2.4 psum.22
  477.8 1.4 convolution_bitcast_fusion
  479.2 41.4 %psum.23 = f32[4,1,128]{2,1,0:T(1,128)} all-reduce(f32[4,1,128]{2,1,0:T(1,128)S(1)} %convolution_bitcast_fusion), channel_id=1, replica_groups=mesh['gen'=4,'user'=4,'cand'=2] {'gen','user'}, use_global_device_ids=true, to_apply=%region_11.12 | all-reduce | flops 512 | bytes 4096 | tf_op jit(solution)/shard_map/psum | solution.py:85
  (25 shorter events, 0.6 us)
Async XLA Ops:
  6.5 439.7 %copy-start = (bf16[1024,1024]{1,0:T(8,128)(2,1)S(1)}, bf16[1024,1024]{1,0:T(8,128)(2,1)}, u32[]{:S(2)}) copy-start(bf16[1024,1024]{1,0:T(8,128)(2,1)} %param.16) | copy-start | bytes 6291460
  6.5 30.8 %all-gather.6.cloned.1.call-start = ((), (), s32[]{:S(2)}) async-start(), calls=%async_computation.2 | async-start | bytes 12582912 | tf_op jit(solution)/shard_map/all_gather | solution.py:50
  6.5 3.6 copy-start.1
  14.6 104.6 %all-gather.8.cloned.1.call-start = ((), (), s32[]{:S(2)}) async-start(), calls=%async_computation.3 | async-start | bytes 9175040 | tf_op jit(solution)/shard_map/all_gather | solution.py:22
  17.5 182.5 %all-gather.10.cloned.1.call-start = ((), (), s32[]{:S(2)}) async-start(), calls=%async_computation.4 | async-start | bytes 9175040 | tf_op jit(solution)/shard_map/all_gather | solution.py:23
  20.6 260.1 %all-gather.12.cloned.1.call-start = ((), (), s32[]{:S(2)}) async-start(), calls=%async_computation.5 | async-start | bytes 9175040 | tf_op jit(solution)/shard_map/all_gather | solution.py:55
  23.5 331.3 %reduce-scatter.3.cloned.1.call-start = ((), (), s32[]{:S(2)}) async-start(), calls=%async_computation.6 | async-start | bytes 6291456 | tf_op jit(solution)/shard_map/reduce_scatter | solution.py:59
  342.6 59.6 %reduce-scatter.5.cloned.1.call-start = ((), (), s32[]{:S(2)}) async-start(), calls=%async_computation.7 | async-start | bytes 2621440 | tf_op jit(solution)/shard_map/reduce_scatter | solution.py:60
  354.8 88.2 %all-reduce.2.cloned.1.call-start = ((), (), s32[]{:S(2)}) async-start(), calls=%async_computation.8 | async-start | bytes 1048576 | tf_op jit(solution)/shard_map/psum | solution.py:66
  367.6 78.5 %copy-start.2 = (s32[256]{0:T(256)S(1)}, s32[256]{0:T(256)}, u32[]{:S(2)}) copy-start(s32[256]{0:T(256)} %param.17) | copy-start | bytes 3076
  405.3 67.6 %all-gather.14.cloned.1.call-start = ((), (), s32[]{:S(2)}) async-start(), calls=%async_computation.9 | async-start | bytes 1310720 | tf_op jit(solution)/shard_map/all_gather | solution.py:68
Sparse Core Ops, SparseCore 0:
  14.7 22.5 all-gather.5
  39.1 80.0 all-gather.7
  121.1 78.8 all-gather.9
  201.7 78.8 all-gather.11
  342.7 12.0 reduce-scatter.2
  357.1 45.1 reduce-scatter.4
  405.4 37.5 all-reduce.1
  446.2 26.6 all-gather.13
where the time goes:
time: 529 us; the launch traced here: 527 us
  waiting for transfers between devices  349 us (66%)
  matrix products  51.4 us (10%)
  blocking collectives  43.8 us (8%)
  other arithmetic  35.2 us (7%)
  local copies, waits for them, and re-layouts  34.1 us (6%)
  between operations  13.5 us (3%)
    all_gather x1, waiting for transfers between devices, project_in(): gate = add_rows(lax.all_gather(gate_part, 'user', axis=0, tiled=True))  81.9 us
    all_gather x1, waiting for transfers between devices, shards(): lax.all_gather(down_part, 'user', axis=1, tiled=True)  80.6 us
    all_gather x1, waiting for transfers between devices, project_in(): up_proj = add_rows(lax.all_gather(up_part, 'user', axis=0, tiled=True))  66.2 us
    psum x1, blocking collectives, shards(): votes = lax.psum(partial_votes, ('gen', 'user'))  41.4 us
    psum x1, waiting for transfers between devices, shards(): embedding = lax.psum(partial_emb, 'gen')  37.7 us
    reduce_scatter x1, waiting for transfers between devices, shards(): lax.psum_scatter(pooled_mlp, 'gen', scatter_dimension=1, tiled=True)  31.7 us
    dot_general x1, matrix products, shards(): jnp.dot(hidden, lax.all_gather(down_part, 'user', axis=1, tiled=True), pr...  27.9 us
    all_gather x1, waiting for transfers between devices, shards(): every_cand = lax.all_gather(candidate, 'user', axis=0, tiled=True)  24.7 us
  transfers between devices with their start and end apart: 8, of which 8 were waited for; matrix products, arithmetic and copies ran while one was open for 8% of the time, Pallas kernels for 0%

commit v1 on v0

v1 whole, which is shorter than its diff:
```python
import functools

import jax
import jax.numpy as jnp
from jax import lax
from jax.experimental import pallas as pl
from jax.experimental.pallas import tpu as pltpu
from jax.sharding import PartitionSpec as P

STEPS = 4
CAP = 8
USERS_DEV = 32
F32 = jnp.float32
BF16 = jnp.bfloat16
MESH = pl.DeviceIdType.MESH


def unit_rows(matrix):
    return (matrix * lax.rsqrt(jnp.sum(matrix * matrix, axis=1, keepdims=True) + 1e-06)).astype(BF16)


def pool_matrix(groups):
    rows = lax.broadcasted_iota(jnp.int32, (groups, groups * STEPS), 0)
    cols = lax.broadcasted_iota(jnp.int32, (groups, groups * STEPS), 1)
    return (cols // STEPS == rows).astype(BF16)


def greet(sizes):
    barrier = pltpu.get_barrier_semaphore()
    count = 0
    for axis, size in sizes:
        me = lax.axis_index(axis)
        for k in range(1, size):
            pl.semaphore_signal(
                barrier, inc=1, device_id={axis: lax.rem(me + k, size)}, device_id_type=MESH
            )
            count += 1
    pl.semaphore_wait(barrier, count)


def push(src, dst, send, recv, axis, peer):
    return pltpu.make_async_remote_copy(
        src_ref=src, dst_ref=dst, send_sem=send, recv_sem=recv,
        device_id={axis: peer}, device_id_type=MESH,
    )


def tail_kernel(
    n_gen, n_user, n_cand, ratio,
    ph_ref, down_ref, proj_ref, ein_ref, enc_ref, cap_ref, out_ref,
    ph_in, e_mine, e_other, sib_in, rs_out, rs_in, zr_out, zr_in, cz, call_in, kern,
    tot_out, tot_in, vote_mine, vote_u_in, vote_g_mine, vote_g_in,
    ph_s, ph_r, sib_s, sib_r, rs_s, rs_r, zr_s, zr_r, cz_s, cz_r, ca_s, ca_r,
    tot_s, tot_r, vu_s, vu_r, vg_s, vg_r,
):
    u = lax.axis_index("user")
    g = lax.axis_index("gen")
    c = lax.axis_index("cand")
    sib = lax.rem(c + 1, n_cand)
    groups = ein_ref.shape[0]
    f_part = ph_ref.shape[1]
    greet((("user", n_user), ("gen", n_gen), ("cand", n_cand)))

    def peer_u(k):
        return lax.rem(u + k, n_user)

    def peer_g(k):
        return lax.rem(g + k, n_gen)

    ph_copy = [
        push(ph_ref, ph_in.at[k - 1], ph_s.at[k - 1], ph_r.at[k - 1], "user", peer_u(k))
        for k in range(1, n_user)
    ]
    for copy in ph_copy:
        copy.start()

    def embed(hidden_sum):
        mixed = jnp.dot(hidden_sum, down_ref[...], preferred_element_type=F32).astype(BF16)
        return jnp.dot(mixed, proj_ref[...], preferred_element_type=F32)

    def split(k, full):
        own = full.reshape(n_cand, groups, full.shape[1])
        e_mine[k] = jnp.where(c == 0, own[0], own[1])
        e_other[k] = jnp.where(c == 0, own[1], own[0]).astype(BF16)

    def sib_copy(k):
        return push(e_other.at[k], sib_in.at[k], sib_s.at[k], sib_r.at[k], "cand", sib)

    def rs_copy(k):
        return push(
            rs_out.at[k - 1], rs_in.at[k - 1], rs_s.at[k - 1], rs_r.at[k - 1],
            "user", lax.rem(u + n_user - k, n_user),
        )

    def step(k, _):
        push(ph_ref, ph_in.at[k - 1], ph_s.at[k - 1], ph_r.at[k - 1], "user", peer_u(k)).wait_recv()
        split(k, embed(ph_in[k - 1]))
        sib_copy(k).start()
        return 0

    split(0, embed(ph_ref[...]))
    sib_copy(0).start()

    def both(k):
        sib_copy(k).wait_recv()
        return e_mine[k] + sib_in[k].astype(F32)

    def home(k, _):
        rs_out[k - 1] = both(k).astype(BF16)
        rs_copy(k).start()
        return 0

    lax.fori_loop(1, n_user, step, 0)
    lax.fori_loop(1, n_user, home, 0)
    total = both(0) + ein_ref[...]
    for k in range(1, n_user):
        rs_copy(k).wait_recv()
        total = total + rs_in[k - 1].astype(F32)

    share = groups // n_gen
    zr_out[...] = total.reshape(n_gen, share, total.shape[1])
    own_sum = zr_out[g]
    zr_copy = []
    for k in range(1, n_gen):
        cz[k] = zr_out[peer_g(k)].astype(BF16)
        copy = push(cz.at[k], zr_in.at[k - 1], zr_s.at[k - 1], zr_r.at[k - 1], "gen", peer_g(k))
        copy.start()
        zr_copy.append(copy)
    for k in range(1, n_gen):
        zr_copy[k - 1].wait_recv()
        own_sum = own_sum + zr_in[k - 1].astype(F32)
    own_sum = own_sum * (1.0 / STEPS)
    cz[0] = unit_rows(own_sum)

    cg_copy = []
    for k in range(1, n_gen):
        copy = push(cz.at[0], call_in.at[0, pl.ds(pl.multiple_of(g * share, share), share)],
                    cz_s.at[k - 1], cz_r.at[k - 1], "gen", peer_g(k))
        copy.start()
        cg_copy.append(copy)
    call_in[0, pl.ds(pl.multiple_of(g * share, share), share)] = cz[0]
    for copy in cg_copy:
        copy.wait_recv()
    ca_copy = []
    for k in range(1, n_user):
        copy = push(call_in.at[0], call_in.at[k], ca_s.at[k - 1], ca_r.at[k - 1], "user", peer_u(k))
        copy.start()
        ca_copy.append(copy)

    def score(k):
        scores = lax.dot_general(
            enc_ref[...], call_in[k], (((1,), (1,)), ((), ())), preferred_element_type=F32
        )
        value = jnp.exp(scores * 60.0)
        kern[k] = value
        return jnp.sum(value, axis=1, keepdims=True)

    totals = score(0)
    for k in range(1, n_user):
        ca_copy[k - 1].wait_recv()
        totals = totals + score(k)
    tot_out[...] = jnp.broadcast_to(totals, tot_out.shape)
    tot_copy = push(tot_out, tot_in, tot_s.at[0], tot_r.at[0], "cand", sib)
    tot_copy.start()
    tot_copy.wait_recv()
    totals = totals + tot_in[:, :1]
    weight = cap_ref[...] / totals * ratio
    for k in range(n_user):
        part = jnp.sum(kern[k] * weight, axis=0, keepdims=True)
        vote_mine[lax.rem(u + n_user - k, n_user)] = jnp.broadcast_to(part, vote_mine.shape[1:])

    vu_copy = []
    for k in range(1, n_user):
        copy = push(vote_mine, vote_u_in.at[k - 1], vu_s.at[k - 1], vu_r.at[k - 1], "user", peer_u(k))
        copy.start()
        vu_copy.append(copy)
    votes = vote_mine[...]
    for k in range(1, n_user):
        vu_copy[k - 1].wait_recv()
        votes = votes + vote_u_in[k - 1]
    vote_g_mine[...] = votes
    vg_copy = []
    for k in range(1, n_gen):
        copy = push(vote_g_mine, vote_g_in.at[k - 1], vg_s.at[k - 1], vg_r.at[k - 1], "gen", peer_g(k))
        copy.start()
        vg_copy.append(copy)
    for k in range(1, n_gen):
        vg_copy[k - 1].wait_recv()
        votes = votes + vote_g_in[k - 1]
    out_ref[...] = votes[:, :1, :]

    for copy in ph_copy + zr_copy + cg_copy + ca_copy + [tot_copy] + vu_copy + vg_copy:
        copy.wait_send()

    def finish(k, _):
        sib_copy(k).wait_send()
        return 0

    def finish_rs(k, _):
        rs_copy(k).wait_send()
        return 0

    lax.fori_loop(0, n_user, finish, 0)
    lax.fori_loop(1, n_user, finish_rs, 0)


def tail(hidden_sum, down_part, proj_user, e_in, encoded, row_cap, ratio):
    n_gen, n_user, n_cand = (lax.axis_size(a) for a in ("gen", "user", "cand"))
    groups, emb = e_in.shape
    rows = encoded.shape[0]
    share = groups // n_gen
    vmem = pltpu.VMEM
    dma = pltpu.SemaphoreType.DMA
    nu, ng = n_user - 1, n_gen - 1
    return pl.pallas_call(
        functools.partial(tail_kernel, n_gen, n_user, n_cand, ratio),
        out_shape=jax.ShapeDtypeStruct((n_user, 1, groups), F32),
        in_specs=[pl.BlockSpec(memory_space=vmem)] * 6,
        out_specs=pl.BlockSpec(memory_space=vmem),
        scratch_shapes=[
            vmem((nu, *hidden_sum.shape), BF16),
            vmem((n_user, groups, emb), F32),
            vmem((n_user, groups, emb), BF16),
            vmem((n_user, groups, emb), BF16),
            vmem((nu, groups, emb), BF16),
            vmem((nu, groups, emb), BF16),
            vmem((n_gen, share, emb), F32),
            vmem((ng, share, emb), BF16),
            vmem((n_gen, share, emb), BF16),
            vmem((n_user, groups, emb), BF16),
            vmem((n_user, rows, groups), F32),
            vmem((rows, 128), F32),
            vmem((rows, 128), F32),
            vmem((n_user, 8, groups), F32),
            vmem((nu, n_user, 8, groups), F32),
            vmem((n_user, 8, groups), F32),
            vmem((ng, n_user, 8, groups), F32),
            dma((nu,)), dma((nu,)),
            dma((n_user,)), dma((n_user,)),
            dma((nu,)), dma((nu,)),
            dma((ng,)), dma((ng,)),
            dma((ng,)), dma((ng,)),
            dma((nu,)), dma((nu,)),
            dma((1,)), dma((1,)),
            dma((nu,)), dma((nu,)),
            dma((ng,)), dma((ng,)),
        ],
        compiler_params=pltpu.CompilerParams(
            collective_id=0, has_side_effects=True, vmem_limit_bytes=56 * 1024 * 1024
        ),
    )(hidden_sum, down_part, proj_user, e_in, encoded, row_cap)


def project_in(inputs, gate_part, up_part):

    def add_rows(piece):
        return jnp.dot(inputs, piece, preferred_element_type=F32)

    gate = add_rows(lax.all_gather(gate_part, "user", axis=0, tiled=True))
    up_proj = add_rows(lax.all_gather(up_part, "user", axis=0, tiled=True))
    return (gate, up_proj)


def proj_of_user(proj_weight):
    n_gen, n_user = lax.axis_size("gen"), lax.axis_size("user")
    per = n_user // n_gen
    rows = proj_weight.shape[0] // per
    slot = lax.rem(lax.axis_index("user"), per)
    piece = lax.dynamic_slice_in_dim(proj_weight, slot * rows, rows, 0)
    pairs = [
        (a * n_user + b, (b // per) * n_user + a * per + b % per)
        for a in range(n_gen) for b in range(n_user)
    ]
    return lax.ppermute(piece, ("gen", "user"), pairs)


def shards(
    states,
    norm_gain,
    gate_weight,
    up_weight,
    down_weight,
    proj_weight,
    private_rows,
    enc_weight,
    user_ids,
):
    tok_rows, width_model = states.shape
    groups = tok_rows // STEPS
    values = states.astype(F32)
    normed = (
        values * lax.rsqrt(jnp.mean(values * values, axis=1, keepdims=True) + 1e-05) * norm_gain
    ).astype(BF16)
    partners = lax.axis_size("cand")
    own_part = lax.axis_index("cand")
    part_width = gate_weight.shape[1] // partners
    gate_part = lax.dynamic_slice_in_dim(gate_weight, own_part * part_width, part_width, 1)
    up_part = lax.dynamic_slice_in_dim(up_weight, own_part * part_width, part_width, 1)
    down_part = lax.dynamic_slice_in_dim(down_weight, own_part * part_width, part_width, 0)
    inputs = lax.all_gather(normed, "cand", axis=0, tiled=True)
    gate, up_proj = project_in(inputs, gate_part, up_part)
    hidden = (jax.nn.silu(gate) * up_proj).astype(BF16)
    hidden_sum = jnp.dot(
        pool_matrix(hidden.shape[0] // STEPS), hidden, preferred_element_type=F32
    ).astype(BF16)

    proj_user = proj_of_user(proj_weight)
    slab_width = proj_weight.shape[0]
    own_cols = lax.dynamic_slice_in_dim(states, lax.axis_index("gen") * slab_width, slab_width, 1)
    pooled_in = jnp.dot(pool_matrix(groups), own_cols, preferred_element_type=F32).astype(BF16)
    e_in = jnp.dot(pooled_in, proj_weight, preferred_element_type=F32)
    encoded = unit_rows(jnp.dot(private_rows, enc_weight, preferred_element_type=F32))
    member = (user_ids[:, None] == jnp.arange(USERS_DEV, dtype=jnp.int32)[None, :]).astype(F32)
    counts = jnp.sum(member, axis=0)
    limit = jnp.minimum(1.0, CAP / jnp.maximum(counts, 1.0))
    row_cap = jnp.sum(member * limit[None, :], axis=1, keepdims=True)
    row_total = private_rows.shape[0] * lax.axis_size("gen") * lax.axis_size("user")
    cand_total = groups * lax.axis_size("user") * partners
    return tail(
        hidden_sum, down_part, proj_user, e_in, encoded, row_cap, cand_total / row_total
    )


def solution(mesh):
    return jax.shard_map(
        shards,
        mesh=mesh,
        in_specs=(
            P(("user", "cand"), None),
            P(),
            P("user", "gen"),
            P("user", "gen"),
            P("gen", "user"),
            P("gen", None),
            P(("gen", "user"), None),
            P(),
            P(("gen", "user")),
        ),
        out_specs=P(None, "cand", None),
        check_vma=False,
    )
```

time: 529 us -> 387 us (0.73)
  waiting for transfers between devices: 349 us -> 222 us
  Pallas kernels: 0 us -> 78.3 us
  blocking collectives: 43.8 us -> 0 us
  other arithmetic: 35.2 us -> 8.78 us
  local copies, waits for them, and re-layouts: 34.1 us -> 11.1 us
  starting transfers between devices: 0.69 us -> 17.5 us
  matrix products: 51.4 us -> 35.6 us
    all_gather x2 -> x0, waiting for transfers between devices: 105 us -> none  [the longest x1 80.6 us: shards(): lax.all_gather(down_part, 'user', axis=1, tiled=True)]
    pallas_call x0 -> x1, Pallas kernels: none -> 78.3 us  [tail(): pl.pallas_call(functools.partial(tail_kernel, n_gen, n_user, n_cand, rati...]
    all_gather x1, waiting for transfers between devices: 81.9 us -> 154 us  [project_in(): gate = add_rows(lax.all_gather(gate_part, 'user', axis=0, tiled=True))]
    reduce_scatter x2 -> x0, waiting for transfers between devices: 43.9 us -> none  [the longest x1 31.7 us: shards(): lax.psum_scatter(pooled_mlp, 'gen', scatter_dimension=1, tiled=True)]
    psum x2 -> x0, blocking collectives: 43.8 us -> none  [the longest x1 41.4 us: shards(): votes = lax.psum(partial_votes, ('gen', 'user'))]
    psum x1 -> x0, waiting for transfers between devices: 37.7 us -> none  [shards(): embedding = lax.psum(partial_emb, 'gen')]
    reshape x2 -> x0, local copies, waits for them, and re-layouts: 21.9 us -> none  [the longest x1 19 us: shards(): pooled_mlp = jnp.sum(mixed.reshape(-1, STEPS, width_model), axis=1)]
    reduce_sum x3 -> x1, other arithmetic: 19 us -> 0.09 us  [shards(): row_cap = jnp.sum(member * limit[None, :], axis=1, keepdims=True)]
  transfers between devices with their start and end apart: 8 -> 4, of which waited for: 8 -> 2; matrix products, arithmetic and copies ran while one was open for 8% -> 12% of each run, Pallas kernels for 0% -> 0%
where the time goes in v1:
time: 387 us; the launch traced here: 386 us
  waiting for transfers between devices  222 us (57%)
  Pallas kernels  78.3 us (20%)
  matrix products  35.6 us (9%)
  starting transfers between devices  17.5 us (5%)
  between operations  13.1 us (3%)
  local copies, waits for them, and re-layouts  11.1 us (3%)
  other arithmetic  8.78 us (2%)
    all_gather x1, waiting for transfers between devices, project_in(): gate = add_rows(lax.all_gather(gate_part, 'user', axis=0, tiled=True))  154 us
    pallas_call x1, Pallas kernels, tail(): pl.pallas_call(functools.partial(tail_kernel, n_gen, n_user, n_cand, rati...  78.3 us
    all_gather x1, waiting for transfers between devices, project_in(): up_proj = add_rows(lax.all_gather(up_part, 'user', axis=0, tiled=True))  67.6 us
    ppermute x1, starting transfers between devices, proj_of_user(): return lax.ppermute(piece, ('gen', 'user'), pairs)  17.4 us
    dot_general x1, matrix products, shards(): jnp.dot(pool_matrix(hidden.shape[0] // STEPS), hidden, preferred_element_...  16.8 us
    dot_general x1, matrix products, add_rows(): return jnp.dot(inputs, piece, preferred_element_type=F32)  14.7 us
  transfers between devices with their start and end apart: 4, of which 2 were waited for; matrix products, arithmetic and copies ran while one was open for 12% of the time, Pallas kernels for 0%

profile of v1, /device:TPU:0, one launch (start us, length us, event | category | flops | bytes accessed | tf_op | source)
XLA Modules:
  0.0 386.1 jit_solution(1339139471437384)
XLA Ops:
  6.5 0.0 copy-start
  6.5 0.0 all-gather.4.cloned.1.call-start
  6.5 0.0 copy-start.1
  6.5 3.2 fusion
  9.8 0.4 copy-done.1
  10.1 4.4 %fusion.2 = bf16[512,4096]{1,0:T(8,128)(2,1)} fusion(bf16[512,4096]{1,0:T(8,128)(2,1)S(1)} %copy-done.1, f32[4096]{0:T(1024)} %param.10, f32[512]{0:T(512)S(1)} %add_rsqrt_fusion), kind=kLoop, calls=%fused_computation.4 | loop fusion | flops 8388608 | bytes 8407040 | tf_op jit(solution)/shard_map/convert_element_type | solution.py:293
  14.5 0.0 all-gather.4.cloned.1.call-update
  14.5 0.0 all-gather.6.cloned.1.call-start
  14.6 2.9 constant_dynamic-slice_fusion.2
  17.5 0.0 copy-start.3
  17.5 0.0 all-gather.6.cloned.1.call-update
  17.5 0.0 all-gather.8.cloned.1.call-start
  17.5 2.9 constant_dynamic-slice_fusion.1
  20.4 0.0 all-gather.8.cloned.1.call-update
  20.5 17.4 %collective-permute-start = (bf16[1024,1024]{1,0:T(8,128)(2,1)}, bf16[1024,1024]{1,0:T(8,128)(2,1)}, u32[]{:S(2)}, u32[]{:S(2)}) collective-permute-start(bf16[1024,1024]{1,0:T(8,128)(2,1)} %param.14), channel_id=1, source_target_pairs={{0,0},{2,8},{4,16},{6,24},{8,2},{10,10},{12,18},{14,26},{16,4},{18... | collective-permute-start | bytes 6291464 | tf_op jit(solution)/shard_map/ppermute | solution.py:274
  37.9 0.0 copy-done.3
  37.9 0.1 convert_reduce_fusion
  38.0 0.1 select_reduce_fusion
  38.1 0.8 copy.11.cap_ref
  39.0 2.9 constant_dynamic-slice_fusion.down_ref
  41.9 0.0 copy-done
  41.9 0.0 copy-done.2
  41.9 0.8 multiply_reduce_fusion
  42.7 0.9 multiply_convert_fusion.1.enc_ref
  43.6 3.3 fusion.6.ein_ref
  46.9 153.9 %all-gather.6.cloned.1.call-done = bf16[4096,896]{1,0:T(8,128)(2,1)} async-done(((bf16[1024,896]{1,0:T(8,128)(2,1)}), bf16[4096,896]{1,0:T(8,128)(2,1)}) %all-gather.6.cloned.1.call-update) | async-done | bytes 7340048 | tf_op jit(solution)/shard_map/all_gather | solution.py:259
  200.8 14.7 %fusion.27 = f32[1024,896]{1,0:T(8,128)} fusion(bf16[1024,4096]{1,0:T(8,128)(2,1)} %all-gather.4.cloned.1.call-done, bf16[4096,896]{1,0:T(8,128)(2,1)} %all-gather.6.cloned.1.call-done), kind=kOutput, calls=%fused_computation.47 | convolution fusion | flops 7516192768 | bytes 19398656 | tf_op jit(solution)/shard_map/dot_general | solution.py:257
  215.5 67.6 %all-gather.8.cloned.1.call-done = bf16[4096,896]{1,0:T(8,128)(2,1)} async-done(((bf16[1024,896]{1,0:T(8,128)(2,1)}), bf16[4096,896]{1,0:T(8,128)(2,1)}) %all-gather.8.cloned.1.call-update) | async-done | bytes 7340048 | tf_op jit(solution)/shard_map/all_gather | solution.py:260
  283.1 16.8 %fusion.5.ph_ref = bf16[256,896]{1,0:T(8,128)(2,1)} fusion(f32[1024,896]{1,0:T(8,128)} %fusion.27, bf16[1024,4096]{1,0:T(8,128)(2,1)} %all-gather.4.cloned.1.call-done, bf16[4096,896]{1,0:T(8,128)(2,1)} %all-gather.8.cloned.1.call-done, s32[1024]{0:T(1024)S(1)} %get-tuple-element.7, s32[1024]{0:T(1024)S(1)} %get-tuple-element.8, pred[1024]{0:T(1024)(128)(4,1)S(1)} %fusion.20), kind=kOutput, calls=%fused_computation.8 | convolution fusion | flops 7992213504 | bytes 19866624 | tf_op jit(solution)/shard_map/dot_general | solution.py:303
  299.9 0.0 collective-permute-done.proj_ref
  299.9 78.3 %shard_map.91 = f32[4,1,128]{2,1,0:T(1,128)} custom-call(bf16[256,896]{1,0:T(8,128)(2,1)} %fusion.5.ph_ref, bf16[896,1024]{1,0:T(8,128)(2,1)} %constant_dynamic-slice_fusion.down_ref, bf16[1024,1024]{1,0:T(8,128)(2,1)} %collective-permute-done.proj_ref, f32[128,1024]{1,0:T(8,128)} %fusion.6.ein_ref, bf16[256,1024]{1,0:T(8,128)(2,1)} %multiply_convert_fusion.1.enc_ref, ...), custom_call_target="tpu_custom_call" | custom-call | tf_op jit(solution)/shard_map/pallas_call | solution.py:215
  378.3 1.3 copy.13
  (9 shorter events, 0.1 us)
Async XLA Ops:
  6.5 35.3 %copy-start = (bf16[1024,1024]{1,0:T(8,128)(2,1)S(1)}, bf16[1024,1024]{1,0:T(8,128)(2,1)}, u32[]{:S(2)}) copy-start(bf16[1024,1024]{1,0:T(8,128)(2,1)} %param.16) | copy-start | bytes 6291460
  6.5 40.4 %all-gather.4.cloned.1.call-start = ((), (), s32[]{:S(2)}) async-start(), calls=%async_computation | async-start | bytes 12582912 | tf_op jit(solution)/shard_map/all_gather | solution.py:300
  6.5 3.6 copy-start.1
  14.5 186.3 %all-gather.6.cloned.1.call-start = ((), (), s32[]{:S(2)}) async-start(), calls=%async_computation.1 | async-start | bytes 9175040 | tf_op jit(solution)/shard_map/all_gather | solution.py:259
  17.5 20.4 %copy-start.3 = (s32[256]{0:T(256)S(1)}, s32[256]{0:T(256)}, u32[]{:S(2)}) copy-start(s32[256]{0:T(256)} %param.17) | copy-start | bytes 3076
  17.5 265.6 %all-gather.8.cloned.1.call-start = ((), (), s32[]{:S(2)}) async-start(), calls=%async_computation.2 | async-start | bytes 9175040 | tf_op jit(solution)/shard_map/all_gather | solution.py:260
  20.4 21.4 %copy-start.2 = (bf16[256,1024]{1,0:T(8,128)(2,1)S(1)}, bf16[256,1024]{1,0:T(8,128)(2,1)}, u32[]{:S(2)}) copy-start(bf16[256,1024]{1,0:T(8,128)(2,1)} %param.15) | copy-start | bytes 1572868
  20.5 279.5 %collective-permute-start = (bf16[1024,1024]{1,0:T(8,128)(2,1)}, bf16[1024,1024]{1,0:T(8,128)(2,1)}, u32[]{:S(2)}, u32[]{:S(2)}) collective-permute-start(bf16[1024,1024]{1,0:T(8,128)(2,1)} %param.14), channel_id=1, source_target_pairs={{0,0},{2,8},{4,16},{6,24},{8,2},{10,10},{12,18},{14,26},{16,4},{18... | collective-permute-start | bytes 6291464 | tf_op jit(solution)/shard_map/ppermute | solution.py:274
Sparse Core Ops, SparseCore 0:
  14.6 22.5 all-gather.3
  39.1 161.6 all-gather.5
  202.7 80.4 all-gather.7

commit v2 on v1

--- a/solution.py
+++ b/solution.py
@@ -45,12 +45,253 @@
     )
 
 
+def normalise(block, gain):
+    values = block.astype(F32)
+    scale = lax.rsqrt(jnp.mean(values * values, axis=1, keepdims=True) + 1e-05)
+    return (values * scale * gain).astype(BF16)
+
+
+def head_kernel(
+    n_gen, n_user, n_cand, chunks,
+    states_ref, gain_ref, gate_ref, up_ref, ph_ref,
+    wbuf, own_norm, part_raw, part_norm, acc,
+    loc, a_s, a_r, b_s, b_r, c_s, c_r, sa_s, sa_r, sb_s, sb_r, sc_s, sc_r, n_s, n_r, z_s, z_r,
+):
+    u = lax.axis_index("user")
+    g = lax.axis_index("gen")
+    c = lax.axis_index("cand")
+    cols = n_user // 2
+    q, x = u // 2, lax.rem(u, 2)
+    mate = q * 2 + 1 - x
+    gen_mate = (g // 2) * 2 + 1 - lax.rem(g, 2)
+    sib = lax.rem(c + 1, n_cand)
+    tokens, width = states_ref.shape
+    depth, half = wbuf.shape[2], wbuf.shape[3]
+    share = depth // n_cand
+    mine = pl.ds(pl.multiple_of(c * share, share), share)
+    weights = (gate_ref, up_ref)
+
+    def above(dq):
+        return lax.rem(q + dq, cols) * 2 + x
+
+    barrier = pltpu.get_barrier_semaphore()
+    for axis, peer in [("user", mate), ("gen", gen_mate), ("cand", sib)] + [
+        ("user", above(dq)) for dq in range(1, cols)
+    ]:
+        pl.semaphore_signal(barrier, inc=1, device_id={axis: peer}, device_id_type=MESH)
+    pl.semaphore_wait(barrier, cols + 2)
+
+    def part(ref, which, rows):
+        if len(ref.shape) == 3:
+            return ref.at[which] if rows is None else ref.at[which, rows]
+        lanes = pl.ds(pl.multiple_of(which * half, half), half)
+        return ref.at[:, lanes] if rows is None else ref.at[rows, lanes]
+
+    sends = []
+
+    def begin(copy):
+        copy.start()
+        sends.append(copy)
+        return copy
+
+    def to_sib(j, block, send, recv):
+        return begin(push(wbuf.at[j, block, mine], wbuf.at[j, block, mine], send, recv, "cand", sib))
+
+    def send_a(j):
+        return begin(push(part(weights[j], 1 - x, mine), wbuf.at[j, u, mine],
+                          a_s.at[j], a_r.at[j], "user", mate))
+
+    def send_b(j):
+        return [
+            begin(push(part(weights[j], x, mine), wbuf.at[j, u, mine],
+                       b_s.at[j, dq - 1], b_r.at[j, dq - 1], "user", above(dq)))
+            for dq in range(1, cols)
+        ]
+
+    def send_c(j):
+        return [
+            begin(push(wbuf.at[j, mate, mine], wbuf.at[j, mate, mine],
+                       c_s.at[j, dq - 1], c_r.at[j, dq - 1], "user", above(dq)))
+            for dq in range(1, cols)
+        ]
+
+    rows_half = tokens // 2
+    piece = rows_half // chunks
+    first = lax.rem(g, 2)
+
+    def piece_rows(which, i):
+        return pl.ds(pl.multiple_of(which * rows_half + i * piece, piece), piece)
+
+    def send_n(i):
+        return begin(push(states_ref.at[piece_rows(first, i)], part_raw.at[piece_rows(first, i)],
+                          n_s.at[i], n_r.at[i], "user", mate))
+
+    def send_z(i):
+        return begin(push(part_raw.at[piece_rows(first, i)], part_raw.at[piece_rows(first, i)],
+                          z_s.at[i], z_r.at[i], "gen", gen_mate))
+
+    a0, b0 = send_a(0), send_b(0)
+    locals_ = []
+    for j in range(2):
+        copy = pltpu.make_async_copy(part(weights[j], x, None), wbuf.at[j, u], loc.at[j])
+        copy.start()
+        locals_.append(copy)
+
+    step = 64
+
+    def norm_own(i, _):
+        rows = pl.ds(pl.multiple_of(i * step, step), step)
+        own_norm[rows] = normalise(states_ref[rows], gain_ref[...])
+        return 0
+
+    lax.fori_loop(0, tokens // step, norm_own, 0)
+    for copy in locals_:
+        copy.wait()
+
+    def own_block(block, start):
+        lanes = pl.ds(pl.multiple_of(block * depth, depth), depth)
+        for j in range(2):
+            term = jnp.dot(own_norm[:, lanes], wbuf[j, block], preferred_element_type=F32)
+            acc[j] = term if start else acc[j] + term
+
+    own_block(u, True)
+
+    def below(dq):
+        return lax.rem(q + cols - dq, cols) * 2
+
+    sib_a, sib_b, sib_c, c_copies = [], [], [], []
+    a0.wait_recv()
+    a1 = send_a(1)
+    c_copies.append(send_c(0))
+    b1 = send_b(1)
+    sib_a.append(to_sib(0, mate, sa_s.at[0], sa_r.at[0]))
+    for dq in range(1, cols):
+        b0[dq - 1].wait_recv()
+        sib_b.append(to_sib(0, below(dq) + x, sb_s.at[0, dq - 1], sb_r.at[0, dq - 1]))
+    a1.wait_recv()
+    n_copies = [send_n(0)]
+    if chunks > 1:
+        n_copies.append(send_n(1))
+    c_copies.append(send_c(1))
+    sib_a.append(to_sib(1, mate, sa_s.at[1], sa_r.at[1]))
+    for copy in sib_a:
+        copy.wait_recv()
+    own_block(mate, False)
+    z_copies = []
+
+    def pass_on(i):
+        n_copies[i].wait_recv()
+        z_copies.append(send_z(i))
+        if i + 2 < chunks:
+            n_copies.append(send_n(i + 2))
+
+    for dq in range(1, cols):
+        b1[dq - 1].wait_recv()
+        sib_b.append(to_sib(1, below(dq) + x, sb_s.at[1, dq - 1], sb_r.at[1, dq - 1]))
+    pass_on(0)
+    for copy in sib_b:
+        copy.wait_recv()
+    for dq in range(1, cols):
+        own_block(below(dq) + x, False)
+    for j in range(2):
+        if j + 1 < chunks:
+            pass_on(j + 1)
+        for dq in range(1, cols):
+            c_copies[j][dq - 1].wait_recv()
+            sib_c.append(to_sib(j, below(dq) + 1 - x, sc_s.at[j, dq - 1], sc_r.at[j, dq - 1]))
+    for i in range(3, chunks):
+        pass_on(i)
+    for copy in sib_c:
+        copy.wait_recv()
+    for dq in range(1, cols):
+        own_block(below(dq) + 1 - x, False)
+
+    groups = tokens // STEPS
+    out_rows = 2 * piece // STEPS
+    pool = pool_matrix(out_rows)
+
+    def pooled(gate, up):
+        hidden = (jax.nn.silu(gate) * up).astype(BF16)
+        return jnp.dot(pool, hidden, preferred_element_type=F32).astype(BF16)
+
+    def own_out(i, _):
+        rows = pl.ds(pl.multiple_of(i * 2 * piece, 2 * piece), 2 * piece)
+        at = pl.multiple_of(x * groups + i * out_rows, out_rows)
+        ph_ref[pl.ds(at, out_rows)] = pooled(acc[0, rows], acc[1, rows])
+        return 0
+
+    lax.fori_loop(0, tokens // (2 * piece), own_out, 0)
+
+    for i in range(chunks):
+        part_norm[:piece] = normalise(part_raw[piece_rows(first, i)], gain_ref[...])
+        z_copies[i].wait_recv()
+        part_norm[piece:] = normalise(part_raw[piece_rows(1 - first, i)], gain_ref[...])
+        both = []
+        for j in range(2):
+            total = None
+            for block in range(n_user):
+                term = jnp.dot(part_norm[:, block * depth:(block + 1) * depth], wbuf[j, block],
+                               preferred_element_type=F32)
+                total = term if total is None else total + term
+            both.append(total)
+        out = pooled(*both)
+        small = out_rows // 2
+        for k, which in enumerate((first, 1 - first)):
+            at = pl.multiple_of(
+                (1 - x) * groups + which * (rows_half // STEPS) + i * small, small
+            )
+            ph_ref[pl.ds(at, small)] = out[k * small:(k + 1) * small]
+
+    for copy in sends:
+        copy.wait_send()
+
+
+def split_columns(weight):
+    half = weight.shape[1] // 2
+    if half % 128 == 0:
+        return weight
+    return weight.reshape(weight.shape[0], 2, half).transpose(1, 0, 2)
+
+
+def head(states, norm_gain, gate_weight, up_weight):
+    n_gen, n_user, n_cand = (lax.axis_size(a) for a in ("gen", "user", "cand"))
+    tokens, width = states.shape
+    depth, half = gate_weight.shape[0], gate_weight.shape[1] // 2
+    chunks = 4
+    cols = n_user // 2
+    vmem = pltpu.VMEM
+    dma = pltpu.SemaphoreType.DMA
+    many = dma((2, cols - 1))
+    anywhere = pl.BlockSpec(memory_space=pl.ANY)
+    inside = pl.BlockSpec(memory_space=vmem)
+    return pl.pallas_call(
+        functools.partial(head_kernel, n_gen, n_user, n_cand, chunks),
+        out_shape=jax.ShapeDtypeStruct((2 * tokens // STEPS, half), BF16),
+        in_specs=[inside, inside, anywhere, anywhere],
+        out_specs=inside,
+        scratch_shapes=[
+            vmem((2, n_user, depth, half), BF16),
+            vmem((tokens, width), BF16),
+            vmem((tokens, width), BF16),
+            vmem((tokens // chunks, width), BF16),
+            vmem((2, tokens, half), F32),
+            dma((2,)),
+            dma((2,)), dma((2,)), many, many, many, many,
+            dma((2,)), dma((2,)), many, many, many, many,
+            dma((chunks,)), dma((chunks,)), dma((chunks,)), dma((chunks,)),
+        ],
+        compiler_params=pltpu.CompilerParams(
+            collective_id=1, has_side_effects=True, vmem_limit_bytes=56 * 1024 * 1024
+        ),
+    )(states, norm_gain.reshape(1, width), split_columns(gate_weight), split_columns(up_weight))
+
+
 def tail_kernel(
     n_gen, n_user, n_cand, ratio,
     ph_ref, down_ref, proj_ref, ein_ref, enc_ref, cap_ref, out_ref,
-    ph_in, e_mine, e_other, sib_in, rs_out, rs_in, zr_out, zr_in, cz, call_in, kern,
+    proj, ph_in, e_own, rs_out, rs_in, zr_out, zr_in, cz, call_in, kern,
     tot_out, tot_in, vote_mine, vote_u_in, vote_g_mine, vote_g_in,
-    ph_s, ph_r, sib_s, sib_r, rs_s, rs_r, zr_s, zr_r, cz_s, cz_r, ca_s, ca_r,
+    pj_s, pj_r, ph_s, ph_r, rs_s, rs_r, zr_s, zr_r, cz_s, cz_r, ca_s, ca_r,
     tot_s, tot_r, vu_s, vu_r, vg_s, vg_r,
 ):
     u = lax.axis_index("user")
@@ -58,7 +299,9 @@
     c = lax.axis_index("cand")
     sib = lax.rem(c + 1, n_cand)
     groups = ein_ref.shape[0]
-    f_part = ph_ref.shape[1]
+    half = ph_ref.shape[1]
+    cols = n_user // 2
+    q, x = u // 2, lax.rem(u, 2)
     greet((("user", n_user), ("gen", n_gen), ("cand", n_cand)))
 
     def peer_u(k):
@@ -67,55 +310,57 @@
     def peer_g(k):
         return lax.rem(g + k, n_gen)
 
-    ph_copy = [
-        push(ph_ref, ph_in.at[k - 1], ph_s.at[k - 1], ph_r.at[k - 1], "user", peer_u(k))
-        for k in range(1, n_user)
-    ]
-    for copy in ph_copy:
-        copy.start()
-
-    def embed(hidden_sum):
-        mixed = jnp.dot(hidden_sum, down_ref[...], preferred_element_type=F32).astype(BF16)
-        return jnp.dot(mixed, proj_ref[...], preferred_element_type=F32)
-
-    def split(k, full):
-        own = full.reshape(n_cand, groups, full.shape[1])
-        e_mine[k] = jnp.where(c == 0, own[0], own[1])
-        e_other[k] = jnp.where(c == 0, own[1], own[0]).astype(BF16)
-
-    def sib_copy(k):
-        return push(e_other.at[k], sib_in.at[k], sib_s.at[k], sib_r.at[k], "cand", sib)
-
-    def rs_copy(k):
-        return push(
-            rs_out.at[k - 1], rs_in.at[k - 1], rs_s.at[k - 1], rs_r.at[k - 1],
-            "user", lax.rem(u + n_user - k, n_user),
-        )
-
-    def step(k, _):
-        push(ph_ref, ph_in.at[k - 1], ph_s.at[k - 1], ph_r.at[k - 1], "user", peer_u(k)).wait_recv()
-        split(k, embed(ph_in[k - 1]))
-        sib_copy(k).start()
+    def ph_copy(dq, dx):
+        k = dq * 2 + dx - 1
+        peer = lax.rem(q + dq, cols) * 2 + lax.rem(x + dx, 2)
+        return push(ph_ref, ph_in.at[u], ph_s.at[k], ph_r.at[k], "user", peer)
+
+    shifts = [(dq, dx) for dq in range(cols) for dx in range(2)][1:]
+    for shift in shifts:
+        ph_copy(*shift).start()
+    proj_rows = proj_ref.shape[0]
+    own_rows = pl.ds(pl.multiple_of(c * proj_rows, proj_rows), proj_rows)
+    pj_copy = push(proj_ref, proj.at[own_rows], pj_s.at[0], pj_r.at[0], "cand", sib)
+    pj_copy.start()
+    proj[own_rows] = proj_ref[...]
+    ph_in[u] = ph_ref[...]
+    pj_copy.wait_recv()
+
+    def rs_copy(dq, dx):
+        k = dq * 2 + dx - 1
+        peer = lax.rem(q + cols - dq, cols) * 2 + lax.rem(x + dx, 2)
+        return push(rs_out.at[k], rs_in.at[k], rs_s.at[k], rs_r.at[k], "user", peer)
+
+    def embed(dq):
+        there = lax.rem(q + cols - dq, cols) * 2
+        mixed = jnp.dot(ph_in[there], down_ref[:half], preferred_element_type=F32)
+        mixed += jnp.dot(ph_in[there + 1], down_ref[half:], preferred_element_type=F32)
+        full = jnp.dot(mixed.astype(BF16), proj[...], preferred_element_type=F32)
+        near = jnp.where(x == 0, full[:groups], full[groups:])
+        far = jnp.where(x == 0, full[groups:], full[:groups])
+        return near, far
+
+    ph_copy(0, 1).wait_recv()
+    near, far = embed(0)
+    rs_out[0] = far.astype(BF16)
+    rs_copy(0, 1).start()
+    e_own[...] = near + ein_ref[...]
+
+    def step(dq, _):
+        ph_copy(dq, 0).wait_recv()
+        ph_copy(dq, 1).wait_recv()
+        near, far = embed(dq)
+        rs_out[dq * 2 - 1] = near.astype(BF16)
+        rs_copy(dq, 0).start()
+        rs_out[dq * 2] = far.astype(BF16)
+        rs_copy(dq, 1).start()
         return 0
 
-    split(0, embed(ph_ref[...]))
-    sib_copy(0).start()
-
-    def both(k):
-        sib_copy(k).wait_recv()
-        return e_mine[k] + sib_in[k].astype(F32)
-
-    def home(k, _):
-        rs_out[k - 1] = both(k).astype(BF16)
-        rs_copy(k).start()
-        return 0
-
-    lax.fori_loop(1, n_user, step, 0)
-    lax.fori_loop(1, n_user, home, 0)
-    total = both(0) + ein_ref[...]
-    for k in range(1, n_user):
-        rs_copy(k).wait_recv()
-        total = total + rs_in[k - 1].astype(F32)
+    lax.fori_loop(1, cols, step, 0)
+    total = e_own[...]
+    for dq, dx in shifts:
+        rs_copy(dq, dx).wait_recv()
+        total = total + rs_in[dq * 2 + dx - 1].astype(F32)
 
     share = groups // n_gen
     zr_out[...] = total.reshape(n_gen, share, total.shape[1])
@@ -189,22 +434,14 @@
         votes = votes + vote_g_in[k - 1]
     out_ref[...] = votes[:, :1, :]
 
-    for copy in ph_copy + zr_copy + cg_copy + ca_copy + [tot_copy] + vu_copy + vg_copy:
+    for copy in [pj_copy] + zr_copy + cg_copy + ca_copy + [tot_copy] + vu_copy + vg_copy:
         copy.wait_send()
-
-    def finish(k, _):
-        sib_copy(k).wait_send()
-        return 0
-
-    def finish_rs(k, _):
-        rs_copy(k).wait_send()
-        return 0
-
-    lax.fori_loop(0, n_user, finish, 0)
-    lax.fori_loop(1, n_user, finish_rs, 0)
-
-
-def tail(hidden_sum, down_part, proj_user, e_in, encoded, row_cap, ratio):
+    for shift in shifts:
+        ph_copy(*shift).wait_send()
+        rs_copy(*shift).wait_send()
+
+
+def tail(hidden_sum, down_weight, proj_user, e_in, encoded, row_cap, ratio):
     n_gen, n_user, n_cand = (lax.axis_size(a) for a in ("gen", "user", "cand"))
     groups, emb = e_in.shape
     rows = encoded.shape[0]
@@ -218,10 +455,9 @@
         in_specs=[pl.BlockSpec(memory_space=vmem)] * 6,
         out_specs=pl.BlockSpec(memory_space=vmem),
         scratch_shapes=[
-            vmem((nu, *hidden_sum.shape), BF16),
-            vmem((n_user, groups, emb), F32),
-            vmem((n_user, groups, emb), BF16),
-            vmem((n_user, groups, emb), BF16),
+            vmem((n_cand * proj_user.shape[0], emb), BF16),
+            vmem((n_user, *hidden_sum.shape), BF16),
+            vmem((groups, emb), F32),
             vmem((nu, groups, emb), BF16),
             vmem((nu, groups, emb), BF16),
             vmem((n_gen, share, emb), F32),
@@ -235,8 +471,8 @@
             vmem((nu, n_user, 8, groups), F32),
             vmem((n_user, 8, groups), F32),
             vmem((ng, n_user, 8, groups), F32),
+            dma((1,)), dma((1,)),
             dma((nu,)), dma((nu,)),
-            dma((n_user,)), dma((n_user,)),
             dma((nu,)), dma((nu,)),
             dma((ng,)), dma((ng,)),
             dma((ng,)), dma((ng,)),
@@ -248,25 +484,17 @@
         compiler_params=pltpu.CompilerParams(
             collective_id=0, has_side_effects=True, vmem_limit_bytes=56 * 1024 * 1024
         ),
-    )(hidden_sum, down_part, proj_user, e_in, encoded, row_cap)
-
-
-def project_in(inputs, gate_part, up_part):
-
-    def add_rows(piece):
-        return jnp.dot(inputs, piece, preferred_element_type=F32)
-
-    gate = add_rows(lax.all_gather(gate_part, "user", axis=0, tiled=True))
-    up_proj = add_rows(lax.all_gather(up_part, "user", axis=0, tiled=True))
-    return (gate, up_proj)
+    )(hidden_sum, down_weight, proj_user, e_in, encoded, row_cap)
 
 
 def proj_of_user(proj_weight):
     n_gen, n_user = lax.axis_size("gen"), lax.axis_size("user")
     per = n_user // n_gen
     rows = proj_weight.shape[0] // per
+    part = rows // lax.axis_size("cand")
     slot = lax.rem(lax.axis_index("user"), per)
-    piece = lax.dynamic_slice_in_dim(proj_weight, slot * rows, rows, 0)
+    start = slot * rows + lax.axis_index("cand") * part
+    piece = lax.dynamic_slice_in_dim(proj_weight, start, part, 0)
     pairs = [
         (a * n_user + b, (b // per) * n_user + a * per + b % per)
         for a in range(n_gen) for b in range(n_user)
@@ -285,25 +513,9 @@
     enc_weight,
     user_ids,
 ):
-    tok_rows, width_model = states.shape
+    tok_rows = states.shape[0]
     groups = tok_rows // STEPS
-    values = states.astype(F32)
-    normed = (
-        values * lax.rsqrt(jnp.mean(values * values, axis=1, keepdims=True) + 1e-05) * norm_gain
-    ).astype(BF16)
-    partners = lax.axis_size("cand")
-    own_part = lax.axis_index("cand")
-    part_width = gate_weight.shape[1] // partners
-    gate_part = lax.dynamic_slice_in_dim(gate_weight, own_part * part_width, part_width, 1)
-    up_part = lax.dynamic_slice_in_dim(up_weight, own_part * part_width, part_width, 1)
-    down_part = lax.dynamic_slice_in_dim(down_weight, own_part * part_width, part_width, 0)
-    inputs = lax.all_gather(normed, "cand", axis=0, tiled=True)
-    gate, up_proj = project_in(inputs, gate_part, up_part)
-    hidden = (jax.nn.silu(gate) * up_proj).astype(BF16)
-    hidden_sum = jnp.dot(
-        pool_matrix(hidden.shape[0] // STEPS), hidden, preferred_element_type=F32
-    ).astype(BF16)
-
+    hidden_sum = head(states, norm_gain, gate_weight, up_weight)
     proj_user = proj_of_user(proj_weight)
     slab_width = proj_weight.shape[0]
     own_cols = lax.dynamic_slice_in_dim(states, lax.axis_index("gen") * slab_width, slab_width, 1)
@@ -315,9 +527,9 @@
     limit = jnp.minimum(1.0, CAP / jnp.maximum(counts, 1.0))
     row_cap = jnp.sum(member * limit[None, :], axis=1, keepdims=True)
     row_total = private_rows.shape[0] * lax.axis_size("gen") * lax.axis_size("user")
-    cand_total = groups * lax.axis_size("user") * partners
+    cand_total = groups * lax.axis_size("user") * lax.axis_size("cand")
     return tail(
-        hidden_sum, down_part, proj_user, e_in, encoded, row_cap, cand_total / row_total
+        hidden_sum, down_weight, proj_user, e_in, encoded, row_cap, cand_total / row_total
     )
 
 

time: 387 us -> 244 us (0.63)
  waiting for transfers between devices: 222 us -> 0.01 us
  Pallas kernels: 78.3 us -> 233 us
  matrix products: 35.6 us -> 3.44 us
  starting transfers between devices: 17.5 us -> 1.65 us
  between operations: 13.1 us -> 0.06 us
  other arithmetic: 8.78 us -> 1.18 us
  local copies, waits for them, and re-layouts: 11.1 us -> 3.72 us
    all_gather x3 -> x0, waiting for transfers between devices: 222 us -> none  [the longest x1 154 us: project_in(): gate = add_rows(lax.all_gather(gate_part, 'user', axis=0, tiled=True))]
    pallas_call x0 -> x1, Pallas kernels: none -> 153 us  [head(): pl.pallas_call(functools.partial(head_kernel, n_gen, n_user, n_cand, chun...]
    dot_general x2 -> x0, matrix products: 31.5 us -> none  [the longest x1 16.8 us: shards(): jnp.dot(pool_matrix(hidden.shape[0] // STEPS), hidden, preferred_element_...]
    ppermute x1, starting transfers between devices: 17.4 us -> 1.65 us  [proj_of_user(): return lax.ppermute(piece, ('gen', 'user'), pairs)]
    dynamic_slice x3 -> x1, local copies, waits for them, and re-layouts: 8.69 us -> 0.07 us  [proj_of_user(): piece = lax.dynamic_slice_in_dim(proj_weight, start, part, 0)]
    convert_element_type x1 -> x0, other arithmetic: 4.36 us -> none  [shards(): normed = (values * lax.rsqrt(jnp.mean(values * values, axis=1, keepdims=T...]
  transfers between devices with their start and end apart: 4 -> 1, of which waited for: 2 -> 0; matrix products, arithmetic and copies ran while one was open for 12% -> 2% of each run, Pallas kernels for 0% -> 63%
where the time goes in v2:
time: 244 us; the launch traced here: 243 us
  Pallas kernels  233 us (95%)
  local copies, waits for them, and re-layouts  3.72 us (2%)
  matrix products  3.44 us (1%)
    pallas_call x1, Pallas kernels, head(): pl.pallas_call(functools.partial(head_kernel, n_gen, n_user, n_cand, chun...  153 us
    pallas_call x1, Pallas kernels, tail(): pl.pallas_call(functools.partial(tail_kernel, n_gen, n_user, n_cand, rati...  80.3 us
  transfers between devices with their start and end apart: 1, of which 0 were waited for; matrix products, arithmetic and copies ran while one was open for 2% of the time, Pallas kernels for 63%

profile of v2, /device:TPU:0, one launch (start us, length us, event | category | flops | bytes accessed | tf_op | source)
XLA Modules:
  0.0 243.4 jit_solution(7763580873526133750)
XLA Ops:
  0.0 0.0 copy-start
  0.0 0.0 copy-start.3
  0.0 1.6 copy-done
  1.6 0.1 constant_dynamic-slice_fusion
  1.7 1.6 collective-permute-start
  3.3 0.0 copy-done.3
  3.3 0.1 convert_reduce_fusion
  3.5 0.1 select_reduce_fusion
  3.6 0.8 copy.11.cap_ref
  4.3 0.0 copy-start.1
  4.4 0.0 copy-start.2
  4.4 153.0 %shard_map.91.ph_ref = bf16[256,896]{1,0:T(8,128)(2,1)} custom-call(bf16[512,4096]{1,0:T(8,128)(2,1)} %states_ref.1, f32[1,4096]{1,0:T(1,128)} %bitcast.5, bf16[1024,1792]{1,0:T(8,128)(2,1)} %gate_ref.1, bf16[1024,1792]{1,0:T(8,128)(2,1)} %up_ref.1), custom_call_target="tpu_custom_call" | custom-call | tf_op jit(solution)/shard_map/pallas_call | solution.py:267
  157.3 0.0 copy-done.1
  157.3 0.0 copy-done.2
  157.4 0.8 multiply_reduce_fusion
  158.2 0.9 multiply_convert_fusion.enc_ref
  159.1 2.6 %fusion.ein_ref = f32[128,1024]{1,0:T(8,128)} fusion(bf16[1024,1024]{1,0:T(8,128)(2,1)S(1)} %copy-done, bf16[512,4096]{1,0:T(8,128)(2,1)} %states_ref.1, s32[]{:T(128)S(6)} %select_n.13, s32[512]{0:T(512)S(1)} %get-tuple-element.7, s32[512]{0:T(512)S(1)} %get-tuple-element.8, pred[512]{0:T(512)(128)(4,1)S(1)} %fusion.11), kind=kOutput, calls=%fused_computation.1 | convolution fusion | flops 402915328 | bytes 3674628 | tf_op jit(solution)/shard_map/dot_general | solution.py:523
  161.8 0.0 collective-permute-done.proj_ref
  161.8 80.3 %shard_map.92 = f32[4,1,128]{2,1,0:T(1,128)} custom-call(bf16[256,896]{1,0:T(8,128)(2,1)} %shard_map.91.ph_ref, bf16[1792,1024]{1,0:T(8,128)(2,1)} %down_ref.1, bf16[512,1024]{1,0:T(8,128)(2,1)} %collective-permute-done.proj_ref, f32[128,1024]{1,0:T(8,128)} %fusion.ein_ref, bf16[256,1024]{1,0:T(8,128)(2,1)} %multiply_convert_fusion.enc_ref, ...), custom_call_target="tpu_custom_call" | custom-call | tf_op jit(solution)/shard_map/pallas_call | solution.py:452
  242.1 1.3 copy.13
  (4 shorter events, 0.0 us)
Async XLA Ops:
  0.0 1.6 copy-start
  0.0 3.3 %copy-start.3 = (s32[256]{0:T(256)S(1)}, s32[256]{0:T(256)}, u32[]{:S(2)}) copy-start(s32[256]{0:T(256)} %param.17) | copy-start | bytes 3076
  1.7 160.1 %collective-permute-start = (bf16[512,1024]{1,0:T(8,128)(2,1)S(1)}, bf16[512,1024]{1,0:T(8,128)(2,1)}, u32[]{:S(2)}, u32[]{:S(2)}) collective-permute-start(bf16[512,1024]{1,0:T(8,128)(2,1)S(1)} %constant_dynamic-slice_fusion), channel_id=1, source_target_pairs={{0,0},{2,8},{4,16},{6,24},{8,2},{10,10},{12,18},{14,26},{16,4},{18... | collective-permute-start | bytes 3145736 | tf_op jit(solution)/shard_map/ppermute | solution.py:502
  4.3 153.0 %copy-start.1 = (bf16[1024,1024]{1,0:T(8,128)(2,1)S(1)}, bf16[1024,1024]{1,0:T(8,128)(2,1)}, u32[]{:S(2)}) copy-start(bf16[1024,1024]{1,0:T(8,128)(2,1)} %param.16) | copy-start | bytes 6291460
  4.4 153.0 %copy-start.2 = (bf16[256,1024]{1,0:T(8,128)(2,1)S(1)}, bf16[256,1024]{1,0:T(8,128)(2,1)}, u32[]{:S(2)}) copy-start(bf16[256,1024]{1,0:T(8,128)(2,1)} %param.15) | copy-start | bytes 1572868

commit v3 on v2

--- a/solution.py
+++ b/solution.py
@@ -53,9 +53,10 @@
 
 def head_kernel(
     n_gen, n_user, n_cand, chunks,
-    states_ref, gain_ref, gate_ref, up_ref, ph_ref,
-    wbuf, own_norm, part_raw, part_norm, acc,
+    states_ref, gain_ref, gate_ref, up_ref, proj_ref, ph_ref, proj_out,
+    wbuf, norm, part_raw, acc,
     loc, a_s, a_r, b_s, b_r, c_s, c_r, sa_s, sa_r, sb_s, sb_r, sc_s, sc_r, n_s, n_r, z_s, z_r,
+    p_s, p_r,
 ):
     u = lax.axis_index("user")
     g = lax.axis_index("gen")
@@ -70,16 +71,15 @@
     share = depth // n_cand
     mine = pl.ds(pl.multiple_of(c * share, share), share)
     weights = (gate_ref, up_ref)
+    others = range(1, cols)
 
     def above(dq):
         return lax.rem(q + dq, cols) * 2 + x
 
-    barrier = pltpu.get_barrier_semaphore()
-    for axis, peer in [("user", mate), ("gen", gen_mate), ("cand", sib)] + [
-        ("user", above(dq)) for dq in range(1, cols)
-    ]:
-        pl.semaphore_signal(barrier, inc=1, device_id={axis: peer}, device_id_type=MESH)
-    pl.semaphore_wait(barrier, cols + 2)
+    def below(dq):
+        return lax.rem(q + cols - dq, cols) * 2
+
+    greet((("user", n_user), ("gen", n_gen), ("cand", n_cand)))
 
     def part(ref, which, rows):
         if len(ref.shape) == 3:
@@ -105,14 +105,14 @@
         return [
             begin(push(part(weights[j], x, mine), wbuf.at[j, u, mine],
                        b_s.at[j, dq - 1], b_r.at[j, dq - 1], "user", above(dq)))
-            for dq in range(1, cols)
+            for dq in others
         ]
 
     def send_c(j):
         return [
             begin(push(wbuf.at[j, mate, mine], wbuf.at[j, mate, mine],
                        c_s.at[j, dq - 1], c_r.at[j, dq - 1], "user", above(dq)))
-            for dq in range(1, cols)
+            for dq in others
         ]
 
     rows_half = tokens // 2
@@ -129,6 +129,36 @@
     def send_z(i):
         return begin(push(part_raw.at[piece_rows(first, i)], part_raw.at[piece_rows(first, i)],
                           z_s.at[i], z_r.at[i], "gen", gen_mate))
+
+    per = n_user // n_gen
+    owner = u // per
+    far = jnp.where(g > owner, g - owner, owner - g)
+    p_rows = proj_out.shape[0]
+    p_at = pl.ds(pl.multiple_of(lax.rem(u, per) * (n_cand * p_rows) + c * p_rows, p_rows), p_rows)
+
+    def proj_up():
+        return push(proj_out, proj_out, p_s.at[0], p_r.at[0], "gen", lax.rem(g + 1, n_gen))
+
+    def proj_down():
+        return push(proj_out, proj_out, p_s.at[1], p_r.at[0], "gen", lax.rem(g + n_gen - 1, n_gen))
+
+    goes_up = jnp.logical_and(g >= owner, g < n_gen - 1)
+    goes_down = jnp.logical_and(g <= owner, g > 0)
+
+    def proj_pass():
+        @pl.when(goes_up)
+        def _():
+            proj_up().start()
+
+        @pl.when(goes_down)
+        def _():
+            proj_down().start()
+
+    def proj_step(k):
+        @pl.when(far == k)
+        def _():
+            proj_up().wait_recv()
+            proj_pass()
 
     a0, b0 = send_a(0), send_b(0)
     locals_ = []
@@ -137,77 +167,109 @@
         copy.start()
         locals_.append(copy)
 
+    @pl.when(far == 0)
+    def _():
+        copy = pltpu.make_async_copy(proj_ref.at[p_at], proj_out, loc.at[2])
+        copy.start()
+        copy.wait()
+        proj_pass()
+
     step = 64
 
     def norm_own(i, _):
         rows = pl.ds(pl.multiple_of(i * step, step), step)
-        own_norm[rows] = normalise(states_ref[rows], gain_ref[...])
+        norm[rows] = normalise(states_ref[rows], gain_ref[...])
         return 0
+
+    def norm_part(i):
+        n_at = tokens + 2 * i * piece
+        norm[n_at:n_at + piece] = normalise(part_raw[piece_rows(first, i)], gain_ref[...])
+        z_copies[i].wait_recv()
+        norm[n_at + piece:n_at + 2 * piece] = normalise(
+            part_raw[piece_rows(1 - first, i)], gain_ref[...]
+        )
+
+    def dots(j, block, low, high, start=False):
+        lanes = pl.ds(pl.multiple_of(block * depth, depth), depth)
+        term = jnp.dot(norm[low:high, lanes], wbuf[j, block], preferred_element_type=F32)
+        acc[j, low:high] = term if start else acc[j, low:high] + term
 
     lax.fori_loop(0, tokens // step, norm_own, 0)
     for copy in locals_:
         copy.wait()
-
-    def own_block(block, start):
-        lanes = pl.ds(pl.multiple_of(block * depth, depth), depth)
-        for j in range(2):
-            term = jnp.dot(own_norm[:, lanes], wbuf[j, block], preferred_element_type=F32)
-            acc[j] = term if start else acc[j] + term
-
-    own_block(u, True)
-
-    def below(dq):
-        return lax.rem(q + cols - dq, cols) * 2
-
-    sib_a, sib_b, sib_c, c_copies = [], [], [], []
+    for j in range(2):
+        dots(j, u, 0, tokens, True)
+
+    early = tokens + (chunks // 2) * 2 * piece
+    sib_b, n_copies, z_copies = [], [], []
+
+    def pass_n(i):
+        n_copies[i].wait_recv()
+        z_copies.append(send_z(i))
+
     a0.wait_recv()
-    a1 = send_a(1)
-    c_copies.append(send_c(0))
+    n_copies += [send_n(0), send_n(1)]
+    c0 = send_c(0)
     b1 = send_b(1)
-    sib_a.append(to_sib(0, mate, sa_s.at[0], sa_r.at[0]))
-    for dq in range(1, cols):
+    sib_a0 = to_sib(0, mate, sa_s.at[0], sa_r.at[0])
+    for dq in others:
         b0[dq - 1].wait_recv()
         sib_b.append(to_sib(0, below(dq) + x, sb_s.at[0, dq - 1], sb_r.at[0, dq - 1]))
-    a1.wait_recv()
-    n_copies = [send_n(0)]
-    if chunks > 1:
-        n_copies.append(send_n(1))
-    c_copies.append(send_c(1))
-    sib_a.append(to_sib(1, mate, sa_s.at[1], sa_r.at[1]))
-    for copy in sib_a:
-        copy.wait_recv()
-    own_block(mate, False)
-    z_copies = []
-
-    def pass_on(i):
-        n_copies[i].wait_recv()
-        z_copies.append(send_z(i))
-        if i + 2 < chunks:
-            n_copies.append(send_n(i + 2))
-
-    for dq in range(1, cols):
+    pass_n(0)
+    a1 = send_a(1)
+    pass_n(1)
+    n_copies.append(send_n(2))
+    proj_step(1)
+    sib_a0.wait_recv()
+    dots(0, mate, 0, tokens)
+    for dq in others:
         b1[dq - 1].wait_recv()
         sib_b.append(to_sib(1, below(dq) + x, sb_s.at[1, dq - 1], sb_r.at[1, dq - 1]))
-    pass_on(0)
+    a1.wait_recv()
+    n_copies.append(send_n(3))
+    c1 = send_c(1)
+    sib_a1 = to_sib(1, mate, sa_s.at[1], sa_r.at[1])
+    proj_step(2)
     for copy in sib_b:
         copy.wait_recv()
-    for dq in range(1, cols):
-        own_block(below(dq) + x, False)
+    for dq in others:
+        for j in range(2):
+            dots(j, below(dq) + x, 0, tokens)
+    pass_n(2)
+    for i in range(chunks // 2):
+        norm_part(i)
     for j in range(2):
-        if j + 1 < chunks:
-            pass_on(j + 1)
-        for dq in range(1, cols):
-            c_copies[j][dq - 1].wait_recv()
-            sib_c.append(to_sib(j, below(dq) + 1 - x, sc_s.at[j, dq - 1], sc_r.at[j, dq - 1]))
-    for i in range(3, chunks):
-        pass_on(i)
+        dots(j, u, tokens, early, True)
+    sib_c = []
+    for dq in others:
+        c0[dq - 1].wait_recv()
+        sib_c.append(to_sib(0, below(dq) + 1 - x, sc_s.at[0, dq - 1], sc_r.at[0, dq - 1]))
+    dots(0, mate, tokens, early)
+    sib_a1.wait_recv()
+    dots(1, mate, 0, early)
+    pass_n(3)
+    for k in range(3, n_gen):
+        proj_step(k)
+    for dq in others:
+        for j in range(2):
+            dots(j, below(dq) + x, tokens, early)
     for copy in sib_c:
         copy.wait_recv()
-    for dq in range(1, cols):
-        own_block(below(dq) + 1 - x, False)
+    for dq in others:
+        dots(0, below(dq) + 1 - x, 0, early)
+    norm_part(2)
+    sib_c = []
+    for dq in others:
+        c1[dq - 1].wait_recv()
+        sib_c.append(to_sib(1, below(dq) + 1 - x, sc_s.at[1, dq - 1], sc_r.at[1, dq - 1]))
+    for copy in sib_c:
+        copy.wait_recv()
+    for dq in others:
+        dots(1, below(dq) + 1 - x, 0, early)
 
     groups = tokens // STEPS
     out_rows = 2 * piece // STEPS
+    small = out_rows // 2
     pool = pool_matrix(out_rows)
 
     def pooled(gate, up):
@@ -220,30 +282,40 @@
         ph_ref[pl.ds(at, out_rows)] = pooled(acc[0, rows], acc[1, rows])
         return 0
 
-    lax.fori_loop(0, tokens // (2 * piece), own_out, 0)
-
-    for i in range(chunks):
-        part_norm[:piece] = normalise(part_raw[piece_rows(first, i)], gain_ref[...])
-        z_copies[i].wait_recv()
-        part_norm[piece:] = normalise(part_raw[piece_rows(1 - first, i)], gain_ref[...])
-        both = []
-        for j in range(2):
-            total = None
-            for block in range(n_user):
-                term = jnp.dot(part_norm[:, block * depth:(block + 1) * depth], wbuf[j, block],
-                               preferred_element_type=F32)
-                total = term if total is None else total + term
-            both.append(total)
-        out = pooled(*both)
-        small = out_rows // 2
+    def part_out(i, out):
         for k, which in enumerate((first, 1 - first)):
             at = pl.multiple_of(
                 (1 - x) * groups + which * (rows_half // STEPS) + i * small, small
             )
             ph_ref[pl.ds(at, small)] = out[k * small:(k + 1) * small]
 
+    lax.fori_loop(0, tokens // (2 * piece), own_out, 0)
+    for i in range(chunks // 2):
+        rows = slice(tokens + 2 * i * piece, tokens + 2 * (i + 1) * piece)
+        part_out(i, pooled(acc[0, rows], acc[1, rows]))
+    norm_part(3)
+    both = []
+    for j in range(2):
+        total = None
+        for block in range(n_user):
+            term = jnp.dot(norm[early:, block * depth:(block + 1) * depth], wbuf[j, block],
+                           preferred_element_type=F32)
+            total = term if total is None else total + term
+        both.append(total)
+    for i in range(chunks // 2, chunks):
+        rows = slice(2 * i * piece + tokens - early, 2 * (i + 1) * piece + tokens - early)
+        part_out(i, pooled(both[0][rows], both[1][rows]))
+
     for copy in sends:
         copy.wait_send()
+
+    @pl.when(goes_up)
+    def _():
+        proj_up().wait_send()
+
+    @pl.when(goes_down)
+    def _():
+        proj_down().wait_send()
 
 
 def split_columns(weight):
@@ -253,11 +325,12 @@
     return weight.reshape(weight.shape[0], 2, half).transpose(1, 0, 2)
 
 
-def head(states, norm_gain, gate_weight, up_weight):
+def head(states, norm_gain, gate_weight, up_weight, proj_weight):
     n_gen, n_user, n_cand = (lax.axis_size(a) for a in ("gen", "user", "cand"))
     tokens, width = states.shape
     depth, half = gate_weight.shape[0], gate_weight.shape[1] // 2
     chunks = 4
+    proj_rows = proj_weight.shape[0] * n_gen // (n_user * n_cand)
     cols = n_user // 2
     vmem = pltpu.VMEM
     dma = pltpu.SemaphoreType.DMA
@@ -266,24 +339,28 @@
     inside = pl.BlockSpec(memory_space=vmem)
     return pl.pallas_call(
         functools.partial(head_kernel, n_gen, n_user, n_cand, chunks),
-        out_shape=jax.ShapeDtypeStruct((2 * tokens // STEPS, half), BF16),
-        in_specs=[inside, inside, anywhere, anywhere],
-        out_specs=inside,
+        out_shape=(
+            jax.ShapeDtypeStruct((2 * tokens // STEPS, half), BF16),
+            jax.ShapeDtypeStruct((proj_rows, proj_weight.shape[1]), BF16),
+        ),
+        in_specs=[inside, inside, anywhere, anywhere, anywhere],
+        out_specs=(inside, inside),
         scratch_shapes=[
             vmem((2, n_user, depth, half), BF16),
+            vmem((2 * tokens, width), BF16),
             vmem((tokens, width), BF16),
-            vmem((tokens, width), BF16),
-            vmem((tokens // chunks, width), BF16),
-            vmem((2, tokens, half), F32),
-            dma((2,)),
+            vmem((2, tokens + tokens // 2, half), F32),
+            dma((3,)),
             dma((2,)), dma((2,)), many, many, many, many,
             dma((2,)), dma((2,)), many, many, many, many,
             dma((chunks,)), dma((chunks,)), dma((chunks,)), dma((chunks,)),
+            dma((2,)), dma((1,)),
         ],
         compiler_params=pltpu.CompilerParams(
             collective_id=1, has_side_effects=True, vmem_limit_bytes=56 * 1024 * 1024
         ),
-    )(states, norm_gain.reshape(1, width), split_columns(gate_weight), split_columns(up_weight))
+    )(states, norm_gain.reshape(1, width), split_columns(gate_weight), split_columns(up_weight),
+      proj_weight)
 
 
 def tail_kernel(
@@ -487,21 +564,6 @@
     )(hidden_sum, down_weight, proj_user, e_in, encoded, row_cap)
 
 
-def proj_of_user(proj_weight):
-    n_gen, n_user = lax.axis_size("gen"), lax.axis_size("user")
-    per = n_user // n_gen
-    rows = proj_weight.shape[0] // per
-    part = rows // lax.axis_size("cand")
-    slot = lax.rem(lax.axis_index("user"), per)
-    start = slot * rows + lax.axis_index("cand") * part
-    piece = lax.dynamic_slice_in_dim(proj_weight, start, part, 0)
-    pairs = [
-        (a * n_user + b, (b // per) * n_user + a * per + b % per)
-        for a in range(n_gen) for b in range(n_user)
-    ]
-    return lax.ppermute(piece, ("gen", "user"), pairs)
-
-
 def shards(
     states,
     norm_gain,
@@ -515,8 +577,7 @@
 ):
     tok_rows = states.shape[0]
     groups = tok_rows // STEPS
-    hidden_sum = head(states, norm_gain, gate_weight, up_weight)
-    proj_user = proj_of_user(proj_weight)
+    hidden_sum, proj_user = head(states, norm_gain, gate_weight, up_weight, proj_weight)
     slab_width = proj_weight.shape[0]
     own_cols = lax.dynamic_slice_in_dim(states, lax.axis_index("gen") * slab_width, slab_width, 1)
     pooled_in = jnp.dot(pool_matrix(groups), own_cols, preferred_element_type=F32).astype(BF16)

time: 244 us -> 208 us (0.85)
  Pallas kernels: 233 us -> 199 us
    pallas_call x1, Pallas kernels: 153 us -> 111 us  [head(): pl.pallas_call(functools.partial(head_kernel, n_gen, n_user, n_cand, chun...]
    pallas_call x1, Pallas kernels: 80.3 us -> 87.4 us  [tail(): pl.pallas_call(functools.partial(tail_kernel, n_gen, n_user, n_cand, rati...]
  transfers between devices with their start and end apart: 1 -> 0, of which waited for: 0 -> 0; matrix products, arithmetic and copies ran while one was open for 2% -> 0% of each run, Pallas kernels for 63% -> 0%
where the time goes in v3:
time: 208 us
  Pallas kernels  199 us (96%)
  matrix products  4.14 us (2%)
  other arithmetic  2.7 us (1%)
    pallas_call x1, Pallas kernels, head(): pl.pallas_call(functools.partial(head_kernel, n_gen, n_user, n_cand, chun...  111 us
    pallas_call x1, Pallas kernels, tail(): pl.pallas_call(functools.partial(tail_kernel, n_gen, n_user, n_cand, rati...  87.4 us

profile of v3, /device:TPU:0, one launch (start us, length us, event | category | flops | bytes accessed | tf_op | source)
XLA Modules:
  0.0 207.6 jit_solution(17210589072551143965)
XLA Ops:
  0.0 0.0 copy-start
  0.0 0.0 copy-start.1
  0.0 0.9 convert_reduce_fusion
  1.0 0.8 select_reduce_fusion
  1.7 0.8 copy.11.cap_ref
  2.5 3.3 %fusion.ein_ref = f32[128,1024]{1,0:T(8,128)} fusion(bf16[1024,1024]{1,0:T(8,128)(2,1)} %proj_ref.1, bf16[512,4096]{1,0:T(8,128)(2,1)} %states_ref.1, s32[]{:T(128)S(6)} %select_n.9, s32[512]{0:T(512)S(1)} %get-tuple-element.11, s32[512]{0:T(512)S(1)} %get-tuple-element.12, pred[512]{0:T(512)(128)(4,1)S(1)} %fusion.11), kind=kOutput, calls=%fused_computation.1 | convolution fusion | flops 402915328 | bytes 3674628 | tf_op jit(solution)/shard_map/dot_general | solution.py:584
  5.9 0.0 copy-done
  5.9 0.0 copy-done.1
  5.9 0.8 multiply_reduce_fusion
  6.7 0.9 multiply_convert_fusion.enc_ref
  7.6 111.3 %shard_map.91 = (bf16[256,896]{1,0:T(8,128)(2,1)}, bf16[512,1024]{1,0:T(8,128)(2,1)}) custom-call(bf16[512,4096]{1,0:T(8,128)(2,1)} %states_ref.1, f32[1,4096]{1,0:T(1,128)} %bitcast.5, bf16[1024,1792]{1,0:T(8,128)(2,1)} %gate_ref.1, bf16[1024,1792]{1,0:T(8,128)(2,1)} %up_ref.1, bf16[1024,1024]{1,0:T(8,128)(2,1)} %proj_ref.1), custom_call_target="tpu_custom_call" | custom-call | tf_op jit(solution)/shard_map/pallas_call | solution.py:340
  118.9 87.4 %shard_map.92 = f32[4,1,128]{2,1,0:T(1,128)} custom-call(bf16[256,896]{1,0:T(8,128)(2,1)} %get-tuple-element.7.ph_ref, bf16[1792,1024]{1,0:T(8,128)(2,1)} %down_ref.1, bf16[512,1024]{1,0:T(8,128)(2,1)} %get-tuple-element.8.proj_ref, f32[128,1024]{1,0:T(8,128)} %fusion.ein_ref, bf16[256,1024]{1,0:T(8,128)(2,1)} %multiply_convert_fusion.enc_ref, ...), custom_call_target="tpu_custom_call" | custom-call | tf_op jit(solution)/shard_map/pallas_call | solution.py:529
  206.4 1.3 copy.13
  (4 shorter events, 0.0 us)
Async XLA Ops:
  0.0 5.9 %copy-start = (bf16[1024,1024]{1,0:T(8,128)(2,1)S(1)}, bf16[1024,1024]{1,0:T(8,128)(2,1)}, u32[]{:S(2)}) copy-start(bf16[1024,1024]{1,0:T(8,128)(2,1)} %param.16) | copy-start | bytes 6291460
  0.0 5.9 %copy-start.1 = (bf16[256,1024]{1,0:T(8,128)(2,1)S(1)}, bf16[256,1024]{1,0:T(8,128)(2,1)}, u32[]{:S(2)}) copy-start(bf16[256,1024]{1,0:T(8,128)(2,1)} %param.15) | copy-start | bytes 1572868

commit v4 on v3

--- a/solution.py
+++ b/solution.py
@@ -9,7 +9,7 @@
 
 STEPS = 4
 CAP = 8
-USERS_DEV = 32
+TAIL_BUFFERS = 13
 F32 = jnp.float32
 BF16 = jnp.bfloat16
 MESH = pl.DeviceIdType.MESH
@@ -51,12 +51,13 @@
     return (values * scale * gain).astype(BF16)
 
 
-def head_kernel(
+def head_part(
     n_gen, n_user, n_cand, chunks,
-    states_ref, gain_ref, gate_ref, up_ref, proj_ref, ph_ref, proj_out,
+    states_ref, gain_ref, gate_ref, up_ref, proj_ref, down_ref, rows_ref, encw_ref,
+    ph_in, proj, e_own, down, encoded,
     wbuf, norm, part_raw, acc,
     loc, a_s, a_r, b_s, b_r, c_s, c_r, sa_s, sa_r, sb_s, sb_r, sc_s, sc_r, n_s, n_r, z_s, z_r,
-    p_s, p_r,
+    p_s, p_r, pj_s, pj_r, ph_s, ph_r,
 ):
     u = lax.axis_index("user")
     g = lax.axis_index("gen")
@@ -133,14 +134,15 @@
     per = n_user // n_gen
     owner = u // per
     far = jnp.where(g > owner, g - owner, owner - g)
-    p_rows = proj_out.shape[0]
+    p_rows = proj.shape[0] // n_cand
+    proj_mine = proj.at[pl.ds(pl.multiple_of(c * p_rows, p_rows), p_rows)]
     p_at = pl.ds(pl.multiple_of(lax.rem(u, per) * (n_cand * p_rows) + c * p_rows, p_rows), p_rows)
 
     def proj_up():
-        return push(proj_out, proj_out, p_s.at[0], p_r.at[0], "gen", lax.rem(g + 1, n_gen))
+        return push(proj_mine, proj_mine, p_s.at[0], p_r.at[0], "gen", lax.rem(g + 1, n_gen))
 
     def proj_down():
-        return push(proj_out, proj_out, p_s.at[1], p_r.at[0], "gen", lax.rem(g + n_gen - 1, n_gen))
+        return push(proj_mine, proj_mine, p_s.at[1], p_r.at[0], "gen", lax.rem(g + n_gen - 1, n_gen))
 
     goes_up = jnp.logical_and(g >= owner, g < n_gen - 1)
     goes_down = jnp.logical_and(g <= owner, g > 0)
@@ -167,9 +169,12 @@
         copy.start()
         locals_.append(copy)
 
+    down_copy = pltpu.make_async_copy(down_ref, down, loc.at[3])
+    down_copy.start()
+
     @pl.when(far == 0)
     def _():
-        copy = pltpu.make_async_copy(proj_ref.at[p_at], proj_out, loc.at[2])
+        copy = pltpu.make_async_copy(proj_ref.at[p_at], proj_mine, loc.at[2])
         copy.start()
         copy.wait()
         proj_pass()
@@ -199,6 +204,13 @@
         copy.wait()
     for j in range(2):
         dots(j, u, 0, tokens, True)
+
+    groups = tokens // STEPS
+    slab = proj_ref.shape[0]
+    own_cols = states_ref[:, pl.ds(pl.multiple_of(g * slab, slab), slab)]
+    pooled_in = jnp.dot(pool_matrix(groups), own_cols, preferred_element_type=F32).astype(BF16)
+    e_own[...] = jnp.dot(pooled_in, proj_ref[...], preferred_element_type=F32)
+    encoded[...] = unit_rows(jnp.dot(rows_ref[...], encw_ref[...], preferred_element_type=F32))
 
     early = tokens + (chunks // 2) * 2 * piece
     sib_b, n_copies, z_copies = [], [], []
@@ -250,6 +262,7 @@
     pass_n(3)
     for k in range(3, n_gen):
         proj_step(k)
+    begin(push(proj_mine, proj_mine, pj_s.at[0], pj_r.at[0], "cand", sib))
     for dq in others:
         for j in range(2):
             dots(j, below(dq) + x, tokens, early)
@@ -267,7 +280,6 @@
     for dq in others:
         dots(1, below(dq) + 1 - x, 0, early)
 
-    groups = tokens // STEPS
     out_rows = 2 * piece // STEPS
     small = out_rows // 2
     pool = pool_matrix(out_rows)
@@ -279,7 +291,7 @@
     def own_out(i, _):
         rows = pl.ds(pl.multiple_of(i * 2 * piece, 2 * piece), 2 * piece)
         at = pl.multiple_of(x * groups + i * out_rows, out_rows)
-        ph_ref[pl.ds(at, out_rows)] = pooled(acc[0, rows], acc[1, rows])
+        ph_in[u, pl.ds(at, out_rows)] = pooled(acc[0, rows], acc[1, rows])
         return 0
 
     def part_out(i, out):
@@ -287,12 +299,24 @@
             at = pl.multiple_of(
                 (1 - x) * groups + which * (rows_half // STEPS) + i * small, small
             )
-            ph_ref[pl.ds(at, small)] = out[k * small:(k + 1) * small]
-
+            ph_in[u, pl.ds(at, small)] = out[k * small:(k + 1) * small]
+
+    def send_ph(part_at, start, size):
+        rows = pl.ds(pl.multiple_of(start, size), size)
+        for dq, dx in [(dq, dx) for dq in range(cols) for dx in range(2)][1:]:
+            k = dq * 2 + dx - 1
+            peer = lax.rem(q + dq, cols) * 2 + lax.rem(x + dx, 2)
+            begin(push(ph_in.at[u, rows], ph_in.at[u, rows], ph_s.at[part_at, k],
+                       ph_r.at[part_at, k], "user", peer))
+
+    quarter = groups // 4
     lax.fori_loop(0, tokens // (2 * piece), own_out, 0)
+    send_ph(0, x * groups, groups)
     for i in range(chunks // 2):
         rows = slice(tokens + 2 * i * piece, tokens + 2 * (i + 1) * piece)
         part_out(i, pooled(acc[0, rows], acc[1, rows]))
+    for k in range(2):
+        send_ph(1 + k, (1 - x) * groups + 2 * k * quarter, quarter)
     norm_part(3)
     both = []
     for j in range(2):
@@ -306,67 +330,29 @@
         rows = slice(2 * i * piece + tokens - early, 2 * (i + 1) * piece + tokens - early)
         part_out(i, pooled(both[0][rows], both[1][rows]))
 
-    for copy in sends:
-        copy.wait_send()
-
-    @pl.when(goes_up)
-    def _():
-        proj_up().wait_send()
-
-    @pl.when(goes_down)
-    def _():
-        proj_down().wait_send()
-
-
-def split_columns(weight):
-    half = weight.shape[1] // 2
-    if half % 128 == 0:
-        return weight
-    return weight.reshape(weight.shape[0], 2, half).transpose(1, 0, 2)
-
-
-def head(states, norm_gain, gate_weight, up_weight, proj_weight):
-    n_gen, n_user, n_cand = (lax.axis_size(a) for a in ("gen", "user", "cand"))
-    tokens, width = states.shape
-    depth, half = gate_weight.shape[0], gate_weight.shape[1] // 2
-    chunks = 4
-    proj_rows = proj_weight.shape[0] * n_gen // (n_user * n_cand)
-    cols = n_user // 2
-    vmem = pltpu.VMEM
-    dma = pltpu.SemaphoreType.DMA
-    many = dma((2, cols - 1))
-    anywhere = pl.BlockSpec(memory_space=pl.ANY)
-    inside = pl.BlockSpec(memory_space=vmem)
-    return pl.pallas_call(
-        functools.partial(head_kernel, n_gen, n_user, n_cand, chunks),
-        out_shape=(
-            jax.ShapeDtypeStruct((2 * tokens // STEPS, half), BF16),
-            jax.ShapeDtypeStruct((proj_rows, proj_weight.shape[1]), BF16),
-        ),
-        in_specs=[inside, inside, anywhere, anywhere, anywhere],
-        out_specs=(inside, inside),
-        scratch_shapes=[
-            vmem((2, n_user, depth, half), BF16),
-            vmem((2 * tokens, width), BF16),
-            vmem((tokens, width), BF16),
-            vmem((2, tokens + tokens // 2, half), F32),
-            dma((3,)),
-            dma((2,)), dma((2,)), many, many, many, many,
-            dma((2,)), dma((2,)), many, many, many, many,
-            dma((chunks,)), dma((chunks,)), dma((chunks,)), dma((chunks,)),
-            dma((2,)), dma((1,)),
-        ],
-        compiler_params=pltpu.CompilerParams(
-            collective_id=1, has_side_effects=True, vmem_limit_bytes=56 * 1024 * 1024
-        ),
-    )(states, norm_gain.reshape(1, width), split_columns(gate_weight), split_columns(up_weight),
-      proj_weight)
-
-
-def tail_kernel(
+    for k in range(2):
+        send_ph(3 + k, (1 - x) * groups + (2 * k + 1) * quarter, quarter)
+    down_copy.wait()
+
+    def finish():
+        for copy in sends:
+            copy.wait_send()
+
+        @pl.when(goes_up)
+        def _():
+            proj_up().wait_send()
+
+        @pl.when(goes_down)
+        def _():
+            proj_down().wait_send()
+
+    return finish
+
+
+def tail_part(
     n_gen, n_user, n_cand, ratio,
-    ph_ref, down_ref, proj_ref, ein_ref, enc_ref, cap_ref, out_ref,
-    proj, ph_in, e_own, rs_out, rs_in, zr_out, zr_in, cz, call_in, kern,
+    ids_col, ids_row, out_ref,
+    ph_in, proj, e_own, down_ref, enc_ref, rs_out, rs_in, zr_out, zr_in, cz, call_in, kern,
     tot_out, tot_in, vote_mine, vote_u_in, vote_g_mine, vote_g_in,
     pj_s, pj_r, ph_s, ph_r, rs_s, rs_r, zr_s, zr_r, cz_s, cz_r, ca_s, ca_r,
     tot_s, tot_r, vu_s, vu_r, vg_s, vg_r,
@@ -375,11 +361,10 @@
     g = lax.axis_index("gen")
     c = lax.axis_index("cand")
     sib = lax.rem(c + 1, n_cand)
-    groups = ein_ref.shape[0]
-    half = ph_ref.shape[1]
+    groups = e_own.shape[0]
+    half = ph_in.shape[2]
     cols = n_user // 2
     q, x = u // 2, lax.rem(u, 2)
-    greet((("user", n_user), ("gen", n_gen), ("cand", n_cand)))
 
     def peer_u(k):
         return lax.rem(u + k, n_user)
@@ -387,21 +372,19 @@
     def peer_g(k):
         return lax.rem(g + k, n_gen)
 
-    def ph_copy(dq, dx):
+    shifts = [(dq, dx) for dq in range(cols) for dx in range(2)][1:]
+    quarter = groups // 4
+
+    def ph_wait(dq, dx):
         k = dq * 2 + dx - 1
-        peer = lax.rem(q + dq, cols) * 2 + lax.rem(x + dx, 2)
-        return push(ph_ref, ph_in.at[u], ph_s.at[k], ph_r.at[k], "user", peer)
-
-    shifts = [(dq, dx) for dq in range(cols) for dx in range(2)][1:]
-    for shift in shifts:
-        ph_copy(*shift).start()
-    proj_rows = proj_ref.shape[0]
-    own_rows = pl.ds(pl.multiple_of(c * proj_rows, proj_rows), proj_rows)
-    pj_copy = push(proj_ref, proj.at[own_rows], pj_s.at[0], pj_r.at[0], "cand", sib)
-    pj_copy.start()
-    proj[own_rows] = proj_ref[...]
-    ph_in[u] = ph_ref[...]
-    pj_copy.wait_recv()
+        for part_at in range(5):
+            rows = pl.ds(0, groups if part_at == 0 else quarter)
+            push(ph_in.at[u, rows], ph_in.at[u, rows], ph_s.at[part_at, k],
+                 ph_r.at[part_at, k], "user", lax.rem(u + 1, n_user)).wait_recv()
+
+    p_rows = proj.shape[0] // n_cand
+    proj_half = proj.at[pl.ds(0, p_rows)]
+    push(proj_half, proj_half, pj_s.at[0], pj_r.at[0], "cand", sib).wait_recv()
 
     def rs_copy(dq, dx):
         k = dq * 2 + dx - 1
@@ -417,15 +400,15 @@
         far = jnp.where(x == 0, full[groups:], full[:groups])
         return near, far
 
-    ph_copy(0, 1).wait_recv()
+    ph_wait(0, 1)
     near, far = embed(0)
     rs_out[0] = far.astype(BF16)
     rs_copy(0, 1).start()
-    e_own[...] = near + ein_ref[...]
+    e_own[...] += near
 
     def step(dq, _):
-        ph_copy(dq, 0).wait_recv()
-        ph_copy(dq, 1).wait_recv()
+        ph_wait(dq, 0)
+        ph_wait(dq, 1)
         near, far = embed(dq)
         rs_out[dq * 2 - 1] = near.astype(BF16)
         rs_copy(dq, 0).start()
@@ -486,7 +469,8 @@
     tot_copy.start()
     tot_copy.wait_recv()
     totals = totals + tot_in[:, :1]
-    weight = cap_ref[...] / totals * ratio
+    counts = jnp.sum((ids_col[...] == ids_row[...]).astype(F32), axis=1, keepdims=True)
+    weight = jnp.minimum(1.0, CAP / counts) / totals * ratio
     for k in range(n_user):
         part = jnp.sum(kern[k] * weight, axis=0, keepdims=True)
         vote_mine[lax.rem(u + n_user - k, n_user)] = jnp.broadcast_to(part, vote_mine.shape[1:])
@@ -511,30 +495,73 @@
         votes = votes + vote_g_in[k - 1]
     out_ref[...] = votes[:, :1, :]
 
-    for copy in [pj_copy] + zr_copy + cg_copy + ca_copy + [tot_copy] + vu_copy + vg_copy:
+    for copy in zr_copy + cg_copy + ca_copy + [tot_copy] + vu_copy + vg_copy:
         copy.wait_send()
     for shift in shifts:
-        ph_copy(*shift).wait_send()
         rs_copy(*shift).wait_send()
 
 
-def tail(hidden_sum, down_weight, proj_user, e_in, encoded, row_cap, ratio):
+def split_columns(weight):
+    half = weight.shape[1] // 2
+    if half % 128 == 0:
+        return weight
+    return weight.reshape(weight.shape[0], 2, half).transpose(1, 0, 2)
+
+
+def fused_kernel(n_gen, n_user, n_cand, chunks, ratio, *refs):
+    ins, refs = refs[:10], refs[10:]
+    out_ref, refs = refs[0], refs[1:]
+    shared, refs = refs[:5], refs[5:]
+    head_own, refs = refs[:23], refs[23:]
+    (pj_s, pj_r, ph_s, ph_r), tail_own = refs[:4], refs[4:]
+    sizes = (n_gen, n_user, n_cand)
+    finish = head_part(*sizes, chunks, *ins[:8], *shared, *head_own, pj_s, pj_r, ph_s, ph_r)
+    tail_part(
+        *sizes, ratio, *ins[8:], out_ref, *shared, *tail_own[:TAIL_BUFFERS],
+        pj_s, pj_r, ph_s, ph_r, *tail_own[TAIL_BUFFERS:],
+    )
+    finish()
+
+
+def fused(states, norm_gain, gate_weight, up_weight, proj_weight, down_weight, private_rows,
+          enc_weight, user_ids, ratio):
     n_gen, n_user, n_cand = (lax.axis_size(a) for a in ("gen", "user", "cand"))
-    groups, emb = e_in.shape
-    rows = encoded.shape[0]
+    tokens, width = states.shape
+    groups = tokens // STEPS
+    depth, half = gate_weight.shape[0], gate_weight.shape[1] // 2
+    emb = proj_weight.shape[1]
+    rows = private_rows.shape[0]
     share = groups // n_gen
+    chunks = 4
+    cols = n_user // 2
+    nu, ng = n_user - 1, n_gen - 1
     vmem = pltpu.VMEM
     dma = pltpu.SemaphoreType.DMA
-    nu, ng = n_user - 1, n_gen - 1
+    many = dma((2, cols - 1))
+    anywhere = pl.BlockSpec(memory_space=pl.ANY)
+    inside = pl.BlockSpec(memory_space=vmem)
     return pl.pallas_call(
-        functools.partial(tail_kernel, n_gen, n_user, n_cand, ratio),
+        functools.partial(fused_kernel, n_gen, n_user, n_cand, chunks, ratio),
         out_shape=jax.ShapeDtypeStruct((n_user, 1, groups), F32),
-        in_specs=[pl.BlockSpec(memory_space=vmem)] * 6,
-        out_specs=pl.BlockSpec(memory_space=vmem),
+        in_specs=[inside, inside, anywhere, anywhere, inside, anywhere] + [inside] * 4,
+        out_specs=inside,
         scratch_shapes=[
-            vmem((n_cand * proj_user.shape[0], emb), BF16),
-            vmem((n_user, *hidden_sum.shape), BF16),
+            vmem((n_user, 2 * groups, half), BF16),
+            vmem((proj_weight.shape[0] * n_gen // n_user, emb), BF16),
             vmem((groups, emb), F32),
+            vmem(down_weight.shape, BF16),
+            vmem((rows, emb), BF16),
+            vmem((2, n_user, depth, half), BF16),
+            vmem((2 * tokens, width), BF16),
+            vmem((tokens, width), BF16),
+            vmem((2, tokens + tokens // 2, half), F32),
+            dma((4,)),
+            dma((2,)), dma((2,)), many, many, many, many,
+            dma((2,)), dma((2,)), many, many, many, many,
+            dma((chunks,)), dma((chunks,)), dma((chunks,)), dma((chunks,)),
+            dma((2,)), dma((1,)),
+            dma((1,)), dma((1,)),
+            dma((5, nu)), dma((5, nu)),
             vmem((nu, groups, emb), BF16),
             vmem((nu, groups, emb), BF16),
             vmem((n_gen, share, emb), F32),
@@ -548,8 +575,6 @@
             vmem((nu, n_user, 8, groups), F32),
             vmem((n_user, 8, groups), F32),
             vmem((ng, n_user, 8, groups), F32),
-            dma((1,)), dma((1,)),
-            dma((nu,)), dma((nu,)),
             dma((nu,)), dma((nu,)),
             dma((ng,)), dma((ng,)),
             dma((ng,)), dma((ng,)),
@@ -559,9 +584,11 @@
             dma((ng,)), dma((ng,)),
         ],
         compiler_params=pltpu.CompilerParams(
-            collective_id=0, has_side_effects=True, vmem_limit_bytes=56 * 1024 * 1024
+            collective_id=0, has_side_effects=True, vmem_limit_bytes=62 * 1024 * 1024
         ),
-    )(hidden_sum, down_weight, proj_user, e_in, encoded, row_cap)
+    )(states, norm_gain.reshape(1, width), split_columns(gate_weight), split_columns(up_weight),
+      proj_weight, down_weight, private_rows, enc_weight,
+      user_ids.reshape(rows, 1), user_ids.reshape(1, rows))
 
 
 def shards(
@@ -575,23 +602,11 @@
     enc_weight,
     user_ids,
 ):
-    tok_rows = states.shape[0]
-    groups = tok_rows // STEPS
-    hidden_sum, proj_user = head(states, norm_gain, gate_weight, up_weight, proj_weight)
-    slab_width = proj_weight.shape[0]
-    own_cols = lax.dynamic_slice_in_dim(states, lax.axis_index("gen") * slab_width, slab_width, 1)
-    pooled_in = jnp.dot(pool_matrix(groups), own_cols, preferred_element_type=F32).astype(BF16)
-    e_in = jnp.dot(pooled_in, proj_weight, preferred_element_type=F32)
-    encoded = unit_rows(jnp.dot(private_rows, enc_weight, preferred_element_type=F32))
-    member = (user_ids[:, None] == jnp.arange(USERS_DEV, dtype=jnp.int32)[None, :]).astype(F32)
-    counts = jnp.sum(member, axis=0)
-    limit = jnp.minimum(1.0, CAP / jnp.maximum(counts, 1.0))
-    row_cap = jnp.sum(member * limit[None, :], axis=1, keepdims=True)
+    groups = states.shape[0] // STEPS
     row_total = private_rows.shape[0] * lax.axis_size("gen") * lax.axis_size("user")
     cand_total = groups * lax.axis_size("user") * lax.axis_size("cand")
-    return tail(
-        hidden_sum, down_weight, proj_user, e_in, encoded, row_cap, cand_total / row_total
-    )
+    return fused(states, norm_gain, gate_weight, up_weight, proj_weight, down_weight,
+                 private_rows, enc_weight, user_ids, cand_total / row_total)
 
 
 def solution(mesh):

time: 208 us -> 190 us (0.913)
  Pallas kernels: 199 us -> 187 us
  matrix products: 4.14 us -> 0 us
  other arithmetic: 2.7 us -> 0 us
    pallas_call x2 -> x1, Pallas kernels: 199 us -> 187 us  [fused(): pl.pallas_call(functools.partial(fused_kernel, n_gen, n_user, n_cand, chu...]
    dot_general x2 -> x0, matrix products: 4.14 us -> none  [the longest x1 3.35 us: shards(): e_in = jnp.dot(pooled_in, proj_weight, preferred_element_type=F32)]
where the time goes in v4:
time: 190 us
  Pallas kernels  187 us (98%)
  local copies, waits for them, and re-layouts  2.7 us (1%)
    pallas_call x1, Pallas kernels, fused(): pl.pallas_call(functools.partial(fused_kernel, n_gen, n_user, n_cand, chu...  187 us

profile of v4, /device:TPU:0, one launch (start us, length us, event | category | flops | bytes accessed | tf_op | source)
XLA Modules:
  0.0 189.6 jit_solution(9893943194741724890)
XLA Ops:
  0.0 1.5 copy.10.refs_8_
  1.5 186.9 %shard_map.91 = f32[4,1,128]{2,1,0:T(1,128)} custom-call(bf16[512,4096]{1,0:T(8,128)(2,1)} %refs_0_.1, f32[1,4096]{1,0:T(1,128)} %bitcast.3, bf16[1024,1792]{1,0:T(8,128)(2,1)} %refs_2_.1, bf16[1024,1792]{1,0:T(8,128)(2,1)} %refs_3_.1, bf16[1024,1024]{1,0:T(8,128)(2,1)} %refs_4_.1, bf16[1792,1024]{1,0:T(8,128)(2,1)} %refs_5_.1, bf16[256,1024]{1,0:T(8,128)(2,1)} %refs_6_.1, ...), custom_call_target="tpu_custom_call" | custom-call | tf_op jit(solution)/shard_map/pallas_call | solution.py:543
  188.3 1.2 copy.12

commit v5 on v4

--- a/solution.py
+++ b/solution.py
@@ -54,10 +54,11 @@
 def head_part(
     n_gen, n_user, n_cand, chunks,
     states_ref, gain_ref, gate_ref, up_ref, proj_ref, down_ref, rows_ref, encw_ref,
-    ph_in, proj, e_own, down, encoded,
+    ids_col, ids_row,
+    ph_in, proj, e_own, down, enc_all, cap_all,
     wbuf, norm, part_raw, acc,
     loc, a_s, a_r, b_s, b_r, c_s, c_r, sa_s, sa_r, sb_s, sb_r, sc_s, sc_r, n_s, n_r, z_s, z_r,
-    p_s, p_r, pj_s, pj_r, ph_s, ph_r,
+    p_s, p_r, en_s, en_r, es_s, es_r, cp_s, cp_r, pj_s, pj_r, ph_s, ph_r,
 ):
     u = lax.axis_index("user")
     g = lax.axis_index("gen")
@@ -210,7 +211,17 @@
     own_cols = states_ref[:, pl.ds(pl.multiple_of(g * slab, slab), slab)]
     pooled_in = jnp.dot(pool_matrix(groups), own_cols, preferred_element_type=F32).astype(BF16)
     e_own[...] = jnp.dot(pooled_in, proj_ref[...], preferred_element_type=F32)
-    encoded[...] = unit_rows(jnp.dot(rows_ref[...], encw_ref[...], preferred_element_type=F32))
+    enc_all[g] = unit_rows(jnp.dot(rows_ref[...], encw_ref[...], preferred_element_type=F32))
+    counts = jnp.sum((ids_col[...] == ids_row[...]).astype(F32), axis=0, keepdims=True)
+    cap_all[g] = jnp.broadcast_to(jnp.minimum(1.0, CAP / counts), cap_all.shape[1:])
+    e_rows = enc_all.shape[1] // n_cand
+    e_mine = pl.ds(pl.multiple_of(c * e_rows, e_rows), e_rows)
+    enc_copies = []
+    for k in range(1, n_gen):
+        peer = lax.rem(g + k, n_gen)
+        enc_copies.append(begin(push(enc_all.at[g, e_mine], enc_all.at[g, e_mine],
+                                     en_s.at[k - 1], en_r.at[k - 1], "gen", peer)))
+        begin(push(cap_all.at[g], cap_all.at[g], cp_s.at[k - 1], cp_r.at[k - 1], "gen", peer))
 
     early = tokens + (chunks // 2) * 2 * piece
     sib_b, n_copies, z_copies = [], [], []
@@ -260,6 +271,11 @@
     sib_a1.wait_recv()
     dots(1, mate, 0, early)
     pass_n(3)
+    for k in range(1, n_gen):
+        enc_copies[k - 1].wait_recv()
+        there = lax.rem(g + n_gen - k, n_gen)
+        begin(push(enc_all.at[there, e_mine], enc_all.at[there, e_mine],
+                   es_s.at[k - 1], es_r.at[k - 1], "cand", sib))
     for k in range(3, n_gen):
         proj_step(k)
     begin(push(proj_mine, proj_mine, pj_s.at[0], pj_r.at[0], "cand", sib))
@@ -351,11 +367,11 @@
 
 def tail_part(
     n_gen, n_user, n_cand, ratio,
-    ids_col, ids_row, out_ref,
-    ph_in, proj, e_own, down_ref, enc_ref, rs_out, rs_in, zr_out, zr_in, cz, call_in, kern,
-    tot_out, tot_in, vote_mine, vote_u_in, vote_g_mine, vote_g_in,
-    pj_s, pj_r, ph_s, ph_r, rs_s, rs_r, zr_s, zr_r, cz_s, cz_r, ca_s, ca_r,
-    tot_s, tot_r, vu_s, vu_r, vg_s, vg_r,
+    out_ref,
+    ph_in, proj, e_own, down_ref, enc_all, cap_all, rs_out, rs_in, zr_out, zr_in, cz, call_in, kern,
+    tot_out, tot_in, tot_sib, vote_mine, vote_u_in, vote_g_all,
+    es_r, cp_r, pj_s, pj_r, ph_s, ph_r, rs_s, rs_r, zr_s, zr_r, ca_s, ca_r,
+    tg_s, tg_r, tot_s, tot_r, vu_s, vu_r, vg_s, vg_r,
 ):
     u = lax.axis_index("user")
     g = lax.axis_index("gen")
@@ -437,65 +453,78 @@
     own_sum = own_sum * (1.0 / STEPS)
     cz[0] = unit_rows(own_sum)
 
-    cg_copy = []
-    for k in range(1, n_gen):
-        copy = push(cz.at[0], call_in.at[0, pl.ds(pl.multiple_of(g * share, share), share)],
-                    cz_s.at[k - 1], cz_r.at[k - 1], "gen", peer_g(k))
-        copy.start()
-        cg_copy.append(copy)
-    call_in[0, pl.ds(pl.multiple_of(g * share, share), share)] = cz[0]
-    for copy in cg_copy:
-        copy.wait_recv()
+    call_in[u] = cz[0]
     ca_copy = []
     for k in range(1, n_user):
-        copy = push(call_in.at[0], call_in.at[k], ca_s.at[k - 1], ca_r.at[k - 1], "user", peer_u(k))
+        copy = push(cz.at[0], call_in.at[u], ca_s.at[k - 1], ca_r.at[k - 1], "user", peer_u(k))
         copy.start()
         ca_copy.append(copy)
-
-    def score(k):
+    for k in range(1, n_gen):
+        half_rows = pl.ds(0, enc_all.shape[1] // n_cand)
+        there = peer_g(k)
+        push(enc_all.at[there, half_rows], enc_all.at[there, half_rows],
+             es_r.at[k - 1], es_r.at[k - 1], "cand", sib).wait_recv()
+        push(cap_all.at[there], cap_all.at[there],
+             cp_r.at[k - 1], cp_r.at[k - 1], "gen", there).wait_recv()
+    for copy in ca_copy:
+        copy.wait_recv()
+    every = call_in[...].reshape(n_user * share, call_in.shape[2])
+    ones = jnp.ones((8, n_user * share), F32)
+    for there in range(n_gen):
         scores = lax.dot_general(
-            enc_ref[...], call_in[k], (((1,), (1,)), ((), ())), preferred_element_type=F32
+            enc_all[there], every, (((1,), (1,)), ((), ())), preferred_element_type=F32
         )
         value = jnp.exp(scores * 60.0)
-        kern[k] = value
-        return jnp.sum(value, axis=1, keepdims=True)
-
-    totals = score(0)
-    for k in range(1, n_user):
-        ca_copy[k - 1].wait_recv()
-        totals = totals + score(k)
-    tot_out[...] = jnp.broadcast_to(totals, tot_out.shape)
-    tot_copy = push(tot_out, tot_in, tot_s.at[0], tot_r.at[0], "cand", sib)
-    tot_copy.start()
-    tot_copy.wait_recv()
-    totals = totals + tot_in[:, :1]
-    counts = jnp.sum((ids_col[...] == ids_row[...]).astype(F32), axis=1, keepdims=True)
-    weight = jnp.minimum(1.0, CAP / counts) / totals * ratio
-    for k in range(n_user):
-        part = jnp.sum(kern[k] * weight, axis=0, keepdims=True)
-        vote_mine[lax.rem(u + n_user - k, n_user)] = jnp.broadcast_to(part, vote_mine.shape[1:])
-
+        kern[there] = value
+        tot_out[there] = lax.dot_general(
+            ones, value, (((1,), (1,)), ((), ())), preferred_element_type=F32,
+            precision=lax.Precision.HIGHEST,
+        )
+    tot_copy = []
+    for k in range(1, n_gen):
+        copy = push(tot_out, tot_in.at[k - 1], tg_s.at[k - 1], tg_r.at[k - 1], "gen", peer_g(k))
+        copy.start()
+        tot_copy.append(copy)
+    totals = tot_out[...]
+    for k in range(1, n_gen):
+        tot_copy[k - 1].wait_recv()
+        totals = totals + tot_in[k - 1]
+    tot_sib[0] = totals
+    copy = push(tot_sib.at[0], tot_sib.at[1], tot_s.at[0], tot_r.at[0], "cand", sib)
+    copy.start()
+    tot_copy.append(copy)
+    copy.wait_recv()
+    weight = cap_all[...] / (totals + tot_sib[1]) * ratio
+    votes = jnp.zeros(vote_mine.shape, F32)
+    for there in range(n_gen):
+        votes = votes + jnp.dot(
+            weight[there], kern[there], preferred_element_type=F32,
+            precision=lax.Precision.HIGHEST,
+        )
+    vote_mine[...] = votes
     vu_copy = []
     for k in range(1, n_user):
         copy = push(vote_mine, vote_u_in.at[k - 1], vu_s.at[k - 1], vu_r.at[k - 1], "user", peer_u(k))
         copy.start()
         vu_copy.append(copy)
-    votes = vote_mine[...]
     for k in range(1, n_user):
         vu_copy[k - 1].wait_recv()
         votes = votes + vote_u_in[k - 1]
-    vote_g_mine[...] = votes
+    vote_g_all[g] = votes
     vg_copy = []
     for k in range(1, n_gen):
-        copy = push(vote_g_mine, vote_g_in.at[k - 1], vg_s.at[k - 1], vg_r.at[k - 1], "gen", peer_g(k))
+        copy = push(vote_g_all.at[g], vote_g_all.at[g], vg_s.at[k - 1], vg_r.at[k - 1], "gen", peer_g(k))
         copy.start()
         vg_copy.append(copy)
-    for k in range(1, n_gen):
-        vg_copy[k - 1].wait_recv()
-        votes = votes + vote_g_in[k - 1]
-    out_ref[...] = votes[:, :1, :]
-
-    for copy in zr_copy + cg_copy + ca_copy + [tot_copy] + vu_copy + vg_copy:
+    for copy in vg_copy:
+        copy.wait_recv()
+    for k in range(n_user):
+        for there in range(n_gen):
+            out_ref[k, :, there * share:(there + 1) * share] = vote_g_all[
+                there, :1, k * share:(k + 1) * share
+            ]
+
+    for copy in zr_copy + ca_copy + tot_copy + vu_copy + vg_copy:
         copy.wait_send()
     for shift in shifts:
         rs_copy(*shift).wait_send()
@@ -511,14 +540,14 @@
 def fused_kernel(n_gen, n_user, n_cand, chunks, ratio, *refs):
     ins, refs = refs[:10], refs[10:]
     out_ref, refs = refs[0], refs[1:]
-    shared, refs = refs[:5], refs[5:]
-    head_own, refs = refs[:23], refs[23:]
+    shared, refs = refs[:6], refs[6:]
+    head_own, refs = refs[:29], refs[29:]
     (pj_s, pj_r, ph_s, ph_r), tail_own = refs[:4], refs[4:]
     sizes = (n_gen, n_user, n_cand)
-    finish = head_part(*sizes, chunks, *ins[:8], *shared, *head_own, pj_s, pj_r, ph_s, ph_r)
+    finish = head_part(*sizes, chunks, *ins, *shared, *head_own, pj_s, pj_r, ph_s, ph_r)
     tail_part(
-        *sizes, ratio, *ins[8:], out_ref, *shared, *tail_own[:TAIL_BUFFERS],
-        pj_s, pj_r, ph_s, ph_r, *tail_own[TAIL_BUFFERS:],
+        *sizes, ratio, out_ref, *shared, *tail_own[:TAIL_BUFFERS],
+        head_own[26], head_own[28], pj_s, pj_r, ph_s, ph_r, *tail_own[TAIL_BUFFERS:],
     )
     finish()
 
@@ -550,7 +579,8 @@
             vmem((proj_weight.shape[0] * n_gen // n_user, emb), BF16),
             vmem((groups, emb), F32),
             vmem(down_weight.shape, BF16),
-            vmem((rows, emb), BF16),
+            vmem((n_gen, rows, emb), BF16),
+            vmem((n_gen, 8, rows), F32),
             vmem((2, n_user, depth, half), BF16),
             vmem((2 * tokens, width), BF16),
             vmem((tokens, width), BF16),
@@ -560,6 +590,7 @@
             dma((2,)), dma((2,)), many, many, many, many,
             dma((chunks,)), dma((chunks,)), dma((chunks,)), dma((chunks,)),
             dma((2,)), dma((1,)),
+            dma((ng,)), dma((ng,)), dma((ng,)), dma((ng,)), dma((ng,)), dma((ng,)),
             dma((1,)), dma((1,)),
             dma((5, nu)), dma((5, nu)),
             vmem((nu, groups, emb), BF16),
@@ -567,18 +598,18 @@
             vmem((n_gen, share, emb), F32),
             vmem((ng, share, emb), BF16),
             vmem((n_gen, share, emb), BF16),
-            vmem((n_user, groups, emb), BF16),
-            vmem((n_user, rows, groups), F32),
-            vmem((rows, 128), F32),
-            vmem((rows, 128), F32),
-            vmem((n_user, 8, groups), F32),
-            vmem((nu, n_user, 8, groups), F32),
-            vmem((n_user, 8, groups), F32),
-            vmem((ng, n_user, 8, groups), F32),
+            vmem((n_user, share, emb), BF16),
+            vmem((n_gen, rows, n_user * share), F32),
+            vmem((n_gen, 8, rows), F32),
+            vmem((ng, n_gen, 8, rows), F32),
+            vmem((2, n_gen, 8, rows), F32),
+            vmem((8, n_user * share), F32),
+            vmem((nu, 8, n_user * share), F32),
+            vmem((n_gen, 8, n_user * share), F32),
             dma((nu,)), dma((nu,)),
             dma((ng,)), dma((ng,)),
+            dma((nu,)), dma((nu,)),
             dma((ng,)), dma((ng,)),
-            dma((nu,)), dma((nu,)),
             dma((1,)), dma((1,)),
             dma((nu,)), dma((nu,)),
             dma((ng,)), dma((ng,)),

time: 190 us -> 181 us (0.953)
  Pallas kernels: 187 us -> 178 us
    pallas_call x1, Pallas kernels: 187 us -> 178 us  [fused(): pl.pallas_call(functools.partial(fused_kernel, n_gen, n_user, n_cand, chu...]
where the time goes in v5:
time: 181 us
  Pallas kernels  178 us (98%)
  local copies, waits for them, and re-layouts  2.7 us (1%)
    pallas_call x1, Pallas kernels, fused(): pl.pallas_call(functools.partial(fused_kernel, n_gen, n_user, n_cand, chu...  178 us

profile of v5, /device:TPU:0, one launch (start us, length us, event | category | flops | bytes accessed | tf_op | source)
XLA Modules:
  0.0 180.5 jit_solution(3536068697440786438)
XLA Ops:
  0.0 1.5 copy.10.refs_8_
  1.5 177.8 %shard_map.91 = f32[4,1,128]{2,1,0:T(1,128)} custom-call(bf16[512,4096]{1,0:T(8,128)(2,1)} %refs_0_.1, f32[1,4096]{1,0:T(1,128)} %bitcast.3, bf16[1024,1792]{1,0:T(8,128)(2,1)} %refs_2_.1, bf16[1024,1792]{1,0:T(8,128)(2,1)} %refs_3_.1, bf16[1024,1024]{1,0:T(8,128)(2,1)} %refs_4_.1, bf16[1792,1024]{1,0:T(8,128)(2,1)} %refs_5_.1, bf16[256,1024]{1,0:T(8,128)(2,1)} %refs_6_.1, ...), custom_call_target="tpu_custom_call" | custom-call | tf_op jit(solution)/shard_map/pallas_call | solution.py:572
  179.3 1.2 copy.12
